TPU v7x, 32 devices: a whole 2x2x4 slice. The times are simulated.
32 devices in a mesh: dp: 4 (over x, core), mp: 8 (over z, y).
Axes of the slice: x: 2, y: 2, z: 4, core: 2. Of those that a mesh axis runs over, the one named last changes fastest.
Arguments:
- tokens: bfloat16 [4704, 768], P(('dp', 'mp')), may hold values from -6 to 6
- crop_kind: int32 [96], P('dp'), may hold values from 0 to 1, as said below
- norm1_gain: float32 [768], replicated, may hold values from 0.1 to 1.9
- norm1_bias: float32 [768], replicated, may hold values from -1.75 to 1.75
- qkv_weight: bfloat16 [3, 768, 768], P(None, None, 'mp'), may hold values from -0.21875 to 0.21875
- qv_bias: float32 [2, 768], P(None, 'mp'), may hold values from -3 to 3
- rel_table: float32 [169, 24], P(None, 'mp'), may hold values from -6 to 6
- proj_weight: bfloat16 [768, 768], P('mp'), may hold values from -0.875 to 0.875
- proj_bias: float32 [768], replicated, may hold values from -1.75 to 1.75
- norm2_gain: float32 [768], replicated, may hold values from 0.1 to 1.9
- norm2_bias: float32 [768], replicated, may hold values from -1.75 to 1.75
- fc1_weight: bfloat16 [768, 3072], P(None, 'mp'), may hold values from -0.21875 to 0.21875
- fc1_bias: float32 [3072], P('mp'), may hold values from -3 to 3
- fc2_weight: bfloat16 [3072, 768], P('mp'), may hold values from -0.109375 to 0.109375
- fc2_bias: float32 [768], replicated, may hold values from -1.75 to 1.75
- out_grad: bfloat16 [4704, 768], P(('dp', 'mp')), may hold values from -6 to 6
Outputs:
- block_out: bfloat16 [4704, 768], P(('dp', 'mp'))
- tokens_grad: bfloat16 [4704, 768], P(('dp', 'mp'))
- norm1_gain_grad: float32 [768], replicated
- norm1_bias_grad: float32 [768], replicated
- qkv_weight_grad: float32 [3, 768, 768], P(None, None, 'mp')
- qv_bias_grad: float32 [2, 768], P(None, 'mp')
- rel_table_grad: float32 [169, 24], P(None, 'mp')
- proj_weight_grad: float32 [768, 768], P('mp')
- proj_bias_grad: float32 [768], replicated
- norm2_gain_grad: float32 [768], replicated
- norm2_bias_grad: float32 [768], replicated
- fc1_weight_grad: float32 [768, 3072], P(None, 'mp')
- fc1_bias_grad: float32 [3072], P('mp')
- fc2_weight_grad: float32 [3072, 768], P('mp')
- fc2_bias_grad: float32 [768], replicated
Inputs may be any that keep to these rules, and one draw needn't show every extreme that they name: `crop_kind`: 0 marks a global crop, whose 49 slots all hold patches; 1 marks a local crop, whose first 9 slots hold patches. Both kinds occur.
All inputs are finite; a program needn't handle non-finite values.
Results may differ from a plain program's by a relative error of at most 0.024.
Values may be sent and summed in bfloat16 or wider, within the bound.
A program may use at most 64 MiB of HBM per device.

v0:
```python
import jax
import jax.numpy as jnp
from jax import lax
from jax.sharding import PartitionSpec as P

HEAD = 32
SIDE = 7
LOCAL_SIDE = 3
WIN = 49


EPSILON = 1e-05
NEG_FILL = -1000000000.0
HIGHEST = lax.Precision.HIGHEST


def normalize(values, gain_vec, shift_vec):
    centre = values - jnp.mean(values, axis=-1, keepdims=True)
    spread = jnp.mean(centre * centre, axis=-1, keepdims=True)
    return centre * lax.rsqrt(spread + EPSILON) * gain_vec + shift_vec


def gelu_tanh(values):
    return jax.nn.gelu(values, approximate=True)


def relative_index(side_len):
    slot_ids = jnp.minimum(jnp.arange(WIN), side_len * side_len - 1)
    slot_row = slot_ids // side_len
    slot_col = slot_ids % side_len
    offset_row = slot_row[:, None] - slot_row[None, :] + SIDE - 1
    offset_col = slot_col[:, None] - slot_col[None, :] + SIDE - 1
    return offset_row * (2 * SIDE - 1) + offset_col


def window_live(kinds):
    return jnp.where(kinds == 0, WIN, LOCAL_SIDE * LOCAL_SIDE)


def table_onehot():
    index_both = jnp.stack([relative_index(SIDE), relative_index(LOCAL_SIDE)]).reshape(2, WIN * WIN)
    entries = jnp.arange((2 * SIDE - 1) ** 2, dtype=jnp.int32)
    return (index_both[:, :, None] == entries[None, None, :]).astype(jnp.float32)


def dot_rows(left, right):
    return lax.dot_general(
        left, right, (((0,), (0,)), ((), ())), preferred_element_type=jnp.float32
    )


def dot_back(left, right):
    return lax.dot_general(
        left, right, (((1,), (1,)), ((), ())), preferred_element_type=jnp.float32
    )


def attention_scores(query_four, key_four, bias_win, key_usable):
    score_raw = jnp.einsum(
        "wqhd,wkhd->whqk", query_four, key_four, preferred_element_type=jnp.float32
    )
    return jnp.where(key_usable[:, None, None, :], score_raw + bias_win, NEG_FILL)


def forward_pass(inputs, kinds, row_live, params, onehot):
    (
        gain_one,
        shift_one,
        qkv_weight,
        qv_bias,
        rel_table,
        proj_weight,
        proj_bias,
        gain_two,
        shift_two,
        fc1_weight,
        fc1_bias,
        fc2_weight,
        fc2_bias,
    ) = params
    head_cols = qkv_weight.shape[2]
    heads_here = head_cols // HEAD
    windows = kinds.shape[0]
    normed_one = normalize(inputs, gain_one, shift_one).astype(jnp.bfloat16)
    rows_one = lax.all_gather(normed_one, "mp", axis=0, tiled=True)
    query_rows = (
        (jnp.dot(rows_one, qkv_weight[0], preferred_element_type=jnp.float32) + qv_bias[0])
        * HEAD ** (-0.5)
    ).astype(jnp.bfloat16)
    key_rows = jnp.dot(rows_one, qkv_weight[1], preferred_element_type=jnp.float32).astype(
        jnp.bfloat16
    )
    value_rows = (
        jnp.dot(rows_one, qkv_weight[2], preferred_element_type=jnp.float32) + qv_bias[1]
    ).astype(jnp.bfloat16)
    bias_both = jnp.einsum("kpt,th->khp", onehot, rel_table, precision=HIGHEST).reshape(
        2, heads_here, WIN, WIN
    )
    is_global = (kinds == 0)[:, None, None, None]
    bias_win = jnp.where(is_global, bias_both[0][None], bias_both[1][None])
    key_usable = jnp.arange(WIN)[None, :] < window_live(kinds)[:, None]
    win_shape = (windows, WIN, heads_here, HEAD)
    scores = attention_scores(
        query_rows.reshape(win_shape), key_rows.reshape(win_shape), bias_win, key_usable
    )
    row_max = jnp.max(scores, axis=-1, keepdims=True)
    log_total = row_max + jnp.log(jnp.sum(jnp.exp(scores - row_max), axis=-1, keepdims=True))
    prob_bf = jnp.exp(scores - log_total).astype(jnp.bfloat16)
    head_out = (
        jnp.einsum(
            "whqk,wkhd->wqhd",
            prob_bf,
            value_rows.reshape(win_shape),
            preferred_element_type=jnp.float32,
        )
        .reshape(windows * WIN, head_cols)
        .astype(jnp.bfloat16)
    )
    attn_branch = lax.psum_scatter(
        jnp.dot(head_out, proj_weight, preferred_element_type=jnp.float32).astype(jnp.bfloat16),
        "mp",
        scatter_dimension=0,
        tiled=True,
    ).astype(jnp.float32)
    middle = inputs + (attn_branch + proj_bias) * row_live
    normed_two = normalize(middle, gain_two, shift_two).astype(jnp.bfloat16)
    rows_two = lax.all_gather(normed_two, "mp", axis=0, tiled=True)
    hidden_pre = jnp.dot(rows_two, fc1_weight, preferred_element_type=jnp.float32) + fc1_bias
    hidden_act = gelu_tanh(hidden_pre).astype(jnp.bfloat16)
    mlp_branch = lax.psum_scatter(
        jnp.dot(hidden_act, fc2_weight, preferred_element_type=jnp.float32).astype(jnp.bfloat16),
        "mp",
        scatter_dimension=0,
        tiled=True,
    ).astype(jnp.float32)
    result = middle + (mlp_branch + fc2_bias) * row_live
    return (
        result,
        middle,
        rows_one,
        query_rows,
        key_rows,
        value_rows,
        bias_win,
        key_usable,
        log_total,
        head_out,
        rows_two,
        hidden_pre,
        hidden_act,
    )


def shards(
    tokens,
    crop_kind,
    norm1_gain,
    norm1_bias,
    qkv_weight,
    qv_bias,
    rel_table,
    proj_weight,
    proj_bias,
    norm2_gain,
    norm2_bias,
    fc1_weight,
    fc1_bias,
    fc2_weight,
    fc2_bias,
    out_grad,
):
    params = (
        norm1_gain,
        norm1_bias,
        qkv_weight,
        qv_bias,
        rel_table,
        proj_weight,
        proj_bias,
        norm2_gain,
        norm2_bias,
        fc1_weight,
        fc1_bias,
        fc2_weight,
        fc2_bias,
    )
    onehot = table_onehot()
    own_rows = tokens.shape[0]
    own_windows = own_rows // WIN
    own_kind = lax.dynamic_slice_in_dim(crop_kind, lax.axis_index("mp") * own_windows, own_windows)
    row_live = (
        (jnp.arange(WIN)[None, :] < window_live(own_kind)[:, None])
        .astype(jnp.float32)
        .reshape(own_rows, 1)
    )
    inputs = tokens.astype(jnp.float32)
    first_pass = forward_pass(inputs, crop_kind, row_live, params, onehot)
    block_out = first_pass[0].astype(jnp.bfloat16)
    saved = forward_pass(inputs, crop_kind, row_live, params, onehot)
    (
        unused_out,
        middle,
        rows_one,
        query_rows,
        key_rows,
        value_rows,
        bias_win,
        key_usable,
        log_total,
        head_out,
        rows_two,
        hidden_pre,
        hidden_act,
    ) = saved
    head_cols = qkv_weight.shape[2]
    heads_here = head_cols // HEAD
    windows = crop_kind.shape[0]
    win_shape = (windows, WIN, heads_here, HEAD)
    upstream = out_grad.astype(jnp.float32)
    mlp_grad = upstream * row_live
    fc2_bias_grad = jnp.sum(mlp_grad, axis=0)
    mlp_grad_rows = lax.all_gather(mlp_grad.astype(jnp.bfloat16), "mp", axis=0, tiled=True)
    fc2_weight_grad = dot_rows(hidden_act, mlp_grad_rows)
    act_grad = dot_back(mlp_grad_rows, fc2_weight)
    unused_act, gelu_pull = jax.vjp(gelu_tanh, hidden_pre)
    pre_grad = gelu_pull(act_grad)[0].astype(jnp.bfloat16)
    fc1_bias_grad = jnp.sum(pre_grad.astype(jnp.float32), axis=0)
    fc1_weight_grad = dot_rows(rows_two, pre_grad)
    normed_two_grad = lax.psum_scatter(
        dot_back(pre_grad, fc1_weight).astype(jnp.bfloat16), "mp", scatter_dimension=0, tiled=True
    ).astype(jnp.float32)
    unused_two, norm_two_pull = jax.vjp(normalize, middle, norm2_gain, norm2_bias)
    middle_grad, norm2_gain_grad, norm2_bias_grad = norm_two_pull(normed_two_grad)
    middle_grad = middle_grad + upstream
    attn_grad = middle_grad * row_live
    proj_bias_grad = jnp.sum(attn_grad, axis=0)
    attn_grad_rows = lax.all_gather(attn_grad.astype(jnp.bfloat16), "mp", axis=0, tiled=True)
    proj_weight_grad = dot_rows(head_out, attn_grad_rows)
    head_grad = dot_back(attn_grad_rows, proj_weight).astype(jnp.bfloat16).reshape(win_shape)
    query_four = query_rows.reshape(win_shape)
    key_four = key_rows.reshape(win_shape)
    scores = attention_scores(query_four, key_four, bias_win, key_usable)
    prob_full = jnp.exp(scores - log_total)
    prob_bf = prob_full.astype(jnp.bfloat16)
    prob_grad = jnp.einsum(
        "wqhd,wkhd->whqk",
        head_grad,
        value_rows.reshape(win_shape),
        preferred_element_type=jnp.float32,
    )
    value_grad = (
        jnp.einsum("whqk,wqhd->wkhd", prob_bf, head_grad, preferred_element_type=jnp.float32)
        .reshape(-1, head_cols)
        .astype(jnp.bfloat16)
    )
    score_grad = prob_full * (prob_grad - jnp.sum(prob_full * prob_grad, axis=-1, keepdims=True))
    is_global = (crop_kind == 0)[:, None, None, None]
    bias_grad = jnp.stack(
        [
            jnp.sum(jnp.where(is_global, score_grad, 0.0), axis=0),
            jnp.sum(jnp.where(is_global, 0.0, score_grad), axis=0),
        ]
    ).reshape(2, heads_here, WIN * WIN)
    rel_table_grad = jnp.einsum("kpt,khp->th", onehot, bias_grad, precision=HIGHEST)
    score_bf = score_grad.astype(jnp.bfloat16)
    query_grad = (
        jnp.einsum(
            "whqk,wkhd->wqhd", score_bf, key_four, preferred_element_type=jnp.float32
        ).reshape(-1, head_cols)
        * HEAD ** (-0.5)
    ).astype(jnp.bfloat16)
    key_grad = (
        jnp.einsum("whqk,wqhd->wkhd", score_bf, query_four, preferred_element_type=jnp.float32)
        .reshape(-1, head_cols)
        .astype(jnp.bfloat16)
    )
    qkv_weight_grad = jnp.stack(
        [
            dot_rows(rows_one, query_grad),
            dot_rows(rows_one, key_grad),
            dot_rows(rows_one, value_grad),
        ]
    )
    qv_bias_grad = jnp.stack(
        [
            jnp.sum(query_grad.astype(jnp.float32), axis=0),
            jnp.sum(value_grad.astype(jnp.float32), axis=0),
        ]
    )
    total = dot_back(query_grad, qkv_weight[0])
    total = total + dot_back(key_grad, qkv_weight[1])
    normed_one_grad = lax.psum_scatter(
        (total + dot_back(value_grad, qkv_weight[2])).astype(jnp.bfloat16),
        "mp",
        scatter_dimension=0,
        tiled=True,
    ).astype(jnp.float32)
    unused_one, norm_one_pull = jax.vjp(normalize, inputs, norm1_gain, norm1_bias)
    input_grad, norm1_gain_grad, norm1_bias_grad = norm_one_pull(normed_one_grad)
    tokens_grad = (input_grad + middle_grad).astype(jnp.bfloat16)
    small_grads = jnp.stack(
        [
            norm1_gain_grad,
            norm1_bias_grad,
            proj_bias_grad,
            norm2_gain_grad,
            norm2_bias_grad,
            fc2_bias_grad,
        ]
    )
    small_grads = lax.psum(small_grads, "mp")
    (
        qkv_weight_grad,
        qv_bias_grad,
        rel_table_grad,
        proj_weight_grad,
        fc1_weight_grad,
        fc1_bias_grad,
        fc2_weight_grad,
        small_grads,
    ) = (
        lax.psum(qkv_weight_grad.astype(jnp.bfloat16), "dp").astype(jnp.float32),
        lax.psum(qv_bias_grad.astype(jnp.bfloat16), "dp").astype(jnp.float32),
        lax.psum(rel_table_grad.astype(jnp.bfloat16), "dp").astype(jnp.float32),
        lax.psum(proj_weight_grad.astype(jnp.bfloat16), "dp").astype(jnp.float32),
        lax.psum(fc1_weight_grad.astype(jnp.bfloat16), "dp").astype(jnp.float32),
        lax.psum(fc1_bias_grad.astype(jnp.bfloat16), "dp").astype(jnp.float32),
        lax.psum(fc2_weight_grad.astype(jnp.bfloat16), "dp").astype(jnp.float32),
        lax.psum(small_grads.astype(jnp.bfloat16), "dp").astype(jnp.float32),
    )
    return (
        block_out,
        tokens_grad,
        small_grads[0],
        small_grads[1],
        qkv_weight_grad,
        qv_bias_grad,
        rel_table_grad,
        proj_weight_grad,
        small_grads[2],
        small_grads[3],
        small_grads[4],
        fc1_weight_grad,
        fc1_bias_grad,
        fc2_weight_grad,
        small_grads[5],
    )


def solution(mesh):
    in_specs = (
        P(("dp", "mp"), None),
        P("dp"),
        P(),
        P(),
        P(None, None, "mp"),
        P(None, "mp"),
        P(None, "mp"),
        P("mp", None),
        P(),
        P(),
        P(),
        P(None, "mp"),
        P("mp"),
        P("mp", None),
        P(),
        P(("dp", "mp"), None),
    )
    out_specs = (
        P(("dp", "mp"), None),
        P(("dp", "mp"), None),
        P(),
        P(),
        P(None, None, "mp"),
        P(None, "mp"),
        P(None, "mp"),
        P("mp", None),
        P(),
        P(),
        P(),
        P(None, "mp"),
        P("mp"),
        P("mp", None),
        P(),
    )
    return jax.shard_map(shards, mesh=mesh, in_specs=in_specs, out_specs=out_specs, check_vma=False)
```

profile of v0, /device:TPU:1, one launch (start us, length us, event | category | flops | bytes accessed | tf_op | source)
XLA Modules:
  0.0 542.7 jit_solution(10992987895275895568)
XLA Ops:
  16.2 43.0 %all-gather.9.cloned.1.call-done = bf16[8,147,768]{2,1,0:T(8,128)(2,1)} async-done(((bf16[1,147,768]{2,1,0:T(8,128)(2,1)}), bf16[8,147,768]{2,1,0:T(8,128)(2,1)}) %all-gather.9.cloned.1.call-update) | async-done | bytes 1806352 | tf_op jit(solution)/shard_map/all_gather | solution.py:85
  59.2 2.1 reshape.423
  69.1 2.2 fusion.95
  77.9 45.6 %fusion = bf16[152,768]{1,0:T(8,128)(2,1)S(1)} fusion(bf16[1176,768]{1,0:T(8,128)(2,1)} %convolution_convert_fusion.2), kind=kCustom, calls=%all-reduce-scatter | all-reduce-scatter fusion | flops 933889 | bytes 2040320
  126.8 2.8 concatenate.2
  133.1 46.9 %all-gather.13.cloned.1.call-done = bf16[8,147,768]{2,1,0:T(8,128)(2,1)} async-done(((bf16[1,147,768]{2,1,0:T(8,128)(2,1)}), bf16[8,147,768]{2,1,0:T(8,128)(2,1)}) %all-gather.13.cloned.1.call-update) | async-done | bytes 1806352 | tf_op jit(solution)/shard_map/all_gather | solution.py:222
  179.9 3.3 reshape.427
  183.2 4.0 fusion.98
  187.2 41.1 %all-gather.11.cloned.1.call-done = bf16[8,147,768]{2,1,0:T(8,128)(2,1)} async-done(((bf16[1,147,768]{2,1,0:T(8,128)(2,1)}), bf16[8,147,768]{2,1,0:T(8,128)(2,1)}) %all-gather.11.cloned.1.call-update) | async-done | bytes 1806352 | tf_op jit(solution)/shard_map/all_gather | solution.py:127
  228.3 3.4 reshape.425
  231.7 6.0 %fusion.91 = (bf16[384]{0:T(512)(128)(2,1)}, bf16[1176,384]{1,0:T(8,128)(2,1)S(1)}, f32[1176,384]{1,0:T(8,128)}) fusion(f32[1176,384]{1,0:T(8,128)} %fusion.98, f32[384]{0:T(512)S(1)} %copy-done.51, bf16[1176,768]{1,0:T(8,128)(2,1)} %reshape.425, bf16[768,384]{1,0:T(8,128)(2,1)S(1)} %copy-done), kind=kOutput, calls=%fused_computation.168 | convolution fusion | flops 703567488 | bytes 6914304 | tf_op jit(solution)/shard_map/dot_general | solution.py:128
  238.6 2.4 convolution_convert_fusion
  241.0 46.1 %fusion.2 = bf16[152,768]{1,0:T(8,128)(2,1)} fusion(bf16[1176,768]{1,0:T(8,128)(2,1)} %convolution_convert_fusion), kind=kCustom, calls=%all-reduce-scatter.2 | all-reduce-scatter fusion | flops 933889 | bytes 2040320
  290.5 4.0 concatenate.4
  299.4 3.9 convolution_convert_fusion.6
  303.3 2.7 convolution_convert_fusion.1
  310.2 37.8 %all-gather.15.cloned.1.call-done = bf16[8,147,768]{2,1,0:T(8,128)(2,1)} async-done(((bf16[1,147,768]{2,1,0:T(8,128)(2,1)}), bf16[8,147,768]{2,1,0:T(8,128)(2,1)}) %all-gather.15.cloned.1.call-update) | async-done | bytes 1806352 | tf_op jit(solution)/shard_map/all_gather | solution.py:237
  348.0 3.4 reshape.429
  351.4 2.8 convolution_convert_fusion.10
  355.6 2.4 reshape.416
  358.0 3.3 fusion.96
  367.1 2.1 fusion.26
  369.2 3.4 fusion.68
  375.6 2.1 fusion.28
  383.2 2.3 fusion.27
  385.5 2.7 convolution_add_fusion.1
  388.9 75.0 %fusion.90 = (bf16[152,768]{1,0:T(8,128)(2,1)S(1)}, bf16[152,768]{1,0:T(8,128)(2,1)S(1)}) fusion(bf16[1176,768]{1,0:T(8,128)(2,1)} %convolution_convert_fusion.1, bf16[1176,768]{1,0:T(8,128)(2,1)S(1)} %fusion.6), kind=kCustom, calls=%all-reduce-scatter.4 | all-reduce-scatter fusion | flops 1867777 | bytes 4080128
  464.0 3.2 collective-permute-start.3
  467.2 3.5 collective-permute-start.1
  470.7 2.4 fusion.30
  476.3 28.1 %psum.63 = bf16[6,768]{1,0:T(8,128)(2,1)S(1)} all-reduce(f32[6,768]{1,0:T(8,128)S(1)} %stack.58), channel_id=1, replica_groups=mesh['dp'=4,'mp'=8] {'mp'}, use_global_device_ids=true, to_apply=%region_21.22 | all-reduce | flops 4608 | bytes 27648 | tf_op jit(solution)/shard_map/psum | solution.py:311
  504.4 21.2 %all-reduce.8 = (bf16[6,768]{1,0:T(8,128)(2,1)S(1)}, bf16[2,96]{1,0:T(2,128)(2,1)S(1)}, bf16[169,3]{0,1:T(4,128)(2,1)S(1)}, bf16[384]{0:T(512)(128)(2,1)S(1)}) all-reduce(bf16[6,768]{1,0:T(8,128)(2,1)S(1)} %psum.63, bf16[2,96]{1,0:T(2,128)(2,1)S(1)} %pad_maximum_fusion.1, ...), channel_id=1, replica_groups=mesh['dp'=4,'mp'=8] {'dp'}, use_global_device_ids=true, to_apply=%region_22.23 | all-reduce | flops 5691 | bytes 22764 | tf_op jit(solution)/shard_map/psum | solution.py:329
  (243 shorter events, 71.9 us)
Async XLA Ops:
  7.2 224.5 %copy-start = (bf16[768,384]{1,0:T(8,128)(2,1)S(1)}, bf16[768,384]{1,0:T(8,128)(2,1)}, u32[]{:S(2)}) copy-start(bf16[768,384]{1,0:T(8,128)(2,1)} %param.27) | copy-start | bytes 1769476
  7.2 6.5 %copy-start.50 = (f32[169,3]{0,1:T(4,128)S(1)}, f32[169,3]{0,1:T(4,128)}, u32[]{:S(2)}) copy-start(f32[169,3]{0,1:T(4,128)} %param.22) | copy-start | bytes 6088
  7.2 8.8 %copy-start.52 = (s32[24]{0:T(128)S(1)}, s32[24]{0:T(128)}, u32[]{:S(2)}) copy-start(s32[24]{0:T(128)} %param.17) | copy-start | bytes 292
  7.2 8.9 %copy-start.45 = (f32[2,96]{1,0:T(2,128)S(1)}, f32[2,96]{1,0:T(2,128)}, u32[]{:S(2)}) copy-start(f32[2,96]{1,0:T(2,128)} %param.21) | copy-start | bytes 2308
  7.2 52.0 %all-gather.9.cloned.1.call-start = ((), (), s32[]{:S(2)}) async-start(), calls=%async_computation | async-start | bytes 2101248 | tf_op jit(solution)/shard_map/all_gather | solution.py:85
  11.4 168.5 %all-gather.13.cloned.1.call-start = ((), (), s32[]{:S(2)}) async-start(), calls=%async_computation.2 | async-start | bytes 2101248 | tf_op jit(solution)/shard_map/all_gather | solution.py:222
  16.1 53.0 %copy-start.46 = (pred[24]{0:T(512)(128)(4,1)}, pred[24]{0:T(512)(128)(4,1)S(1)}, u32[]{:S(2)}) copy-start(pred[24]{0:T(512)(128)(4,1)S(1)} %broadcast_compare_fusion) | copy-start | bytes 76
  16.2 45.1 %copy-start.20 = (bf16[3,768,96]{1,2,0:T(8,128)(2,1)S(1)}, bf16[3,768,96]{1,2,0:T(8,128)(2,1)}, u32[]{:S(2)}) copy-start(bf16[3,768,96]{1,2,0:T(8,128)(2,1)} %param.20) | copy-start | bytes 1327108
  76.0 49.6 %copy-start.48 = (u32[32]{0:T(128)S(1)}, u32[32]{0:T(128)}, u32[]{:S(2)}) copy-start(u32[32]{0:T(128)} %constant.105) | copy-start | bytes 388
  77.8 51.8 %copy-start.3 = (bf16[147,768]{1,0:T(8,128)(2,1)S(1)}, bf16[147,768]{1,0:T(8,128)(2,1)}, u32[]{:S(2)}) copy-start(bf16[147,768]{1,0:T(8,128)(2,1)} %param.16) | copy-start | bytes 677380
  77.8 51.8 %copy-start.29 = (f32[768]{0:T(1024)S(1)}, f32[768]{0:T(1024)}, u32[]{:S(2)}) copy-start(f32[768]{0:T(1024)} %param.24) | copy-start | bytes 9220
  77.8 54.0 %copy-start.32 = (f32[768]{0:T(1024)S(1)}, f32[768]{0:T(1024)}, u32[]{:S(2)}) copy-start(f32[768]{0:T(1024)} %param.25) | copy-start | bytes 9220
  77.8 54.0 %copy-start.42 = (f32[768]{0:T(1024)S(1)}, f32[768]{0:T(1024)}, u32[]{:S(2)}) copy-start(f32[768]{0:T(1024)} %param.26) | copy-start | bytes 9220
  123.5 3.3 collective-permute-start
  131.8 96.5 %all-gather.11.cloned.1.call-start = ((), (), s32[]{:S(2)}) async-start(), calls=%async_computation.1 | async-start | bytes 2101248 | tf_op jit(solution)/shard_map/all_gather | solution.py:127
  132.8 215.2 %all-gather.15.cloned.1.call-start = ((), (), s32[]{:S(2)}) async-start(), calls=%async_computation.3 | async-start | bytes 2101248 | tf_op jit(solution)/shard_map/all_gather | solution.py:237
  187.2 44.4 %copy-start.51 = (f32[384]{0:T(512)S(1)}, f32[384]{0:T(512)}, u32[]{:S(2)}) copy-start(f32[384]{0:T(512)} %param.28) | copy-start | bytes 4612
  287.9 2.6 collective-permute-start.2
  297.4 5.9 %copy-start.38 = (f32[147]{0:T(256)}, f32[147]{0:T(256)S(1)}, u32[]{:S(2)}) copy-start(f32[147]{0:T(256)S(1)} %negate_multiply_fusion.1) | copy-start | bytes 1768
  299.1 230.7 %all-reduce.13.cloned.1.call-start = ((), (), s32[]{:S(2)}) async-start(), calls=%async_computation.4 | async-start | bytes 3538944 | tf_op jit(solution)/shard_map/psum | solution.py:322
  379.0 6.5 %copy-start.14 = (bf16[1176,96]{0,1:T(8,128)(2,1)S(1)}, bf16[1176,96]{0,1:T(8,128)(2,1)}, u32[]{:S(2)}) copy-start(bf16[1176,96]{0,1:T(8,128)(2,1)} %convert_element_type.220) | copy-start | bytes 677380
  388.9 84.2 %copy-start.25 = (bf16[1,768,96]{1,2,0:T(8,128)(2,1)S(1)}, bf16[1,768,96]{1,2,0:T(8,128)(2,1)}, u32[]{:S(2)}) copy-start(bf16[1,768,96]{1,2,0:T(8,128)(2,1)} %fusion.26) | copy-start | bytes 442372
  463.9 11.1 %copy-start.53 = (bf16[1,96]{1,0:T(2,128)(2,1)S(1)}, bf16[1,96]{1,0:T(2,128)(2,1)}, u32[]{:S(2)}) copy-start(bf16[1,96]{1,0:T(2,128)(2,1)} %stack.64) | copy-start | bytes 580
  463.9 11.1 %copy-start.54 = (bf16[1,96]{1,0:T(2,128)(2,1)S(1)}, bf16[1,96]{1,0:T(2,128)(2,1)}, u32[]{:S(2)}) copy-start(bf16[1,96]{1,0:T(2,128)(2,1)} %stack.63) | copy-start | bytes 580
  464.0 11.1 %collective-permute-start.3 = (bf16[35,768]{1,0:T(8,128)(2,1)S(1)}, bf16[35,768]{1,0:T(8,128)(2,1)S(1)}, u32[]{:S(2)}, u32[]{:S(2)}) collective-permute-start(bf16[35,768]{1,0:T(8,128)(2,1)S(1)} %slice.75), channel_id=1, source_target_pairs={{0,1},{1,2},{2,3},{3,4},{4,5},{5,6},{6,7},{8,9},{9,10},{10,11},{11... | collective-permute-start | bytes 161288
  467.2 60.1 %collective-permute-start.1 = (bf16[35,768]{1,0:T(8,128)(2,1)S(1)}, bf16[35,768]{1,0:T(8,128)(2,1)S(1)}, u32[]{:S(2)}, u32[]{:S(2)}) collective-permute-start(bf16[35,768]{1,0:T(8,128)(2,1)S(1)} %slice.73), channel_id=1, source_target_pairs={{0,1},{1,2},{2,3},{3,4},{4,5},{5,6},{6,7},{8,9},{9,10},{10,11},{11... | collective-permute-start | bytes 161288
  475.0 29.4 %copy-start.44 = (bf16[384]{0:T(512)(128)(2,1)S(1)}, bf16[384]{0:T(512)(128)(2,1)}, u32[]{:S(2)}) copy-start(bf16[384]{0:T(512)(128)(2,1)} %get-tuple-element.43) | copy-start | bytes 2308
  475.0 53.4 %copy-start.7 = (f32[147,768]{1,0:T(8,128)S(1)}, f32[147,768]{1,0:T(8,128)}, u32[]{:S(2)}) copy-start(f32[147,768]{1,0:T(8,128)} %copy-done.6) | copy-start | bytes 1354756
  475.1 53.4 %copy-start.16 = (bf16[147,768]{1,0:T(8,128)(2,1)S(1)}, bf16[147,768]{1,0:T(8,128)(2,1)}, u32[]{:S(2)}) copy-start(bf16[147,768]{1,0:T(8,128)(2,1)} %param.31) | copy-start | bytes 677380
  475.1 53.4 %copy-start.39 = (f32[147]{0:T(256)S(1)}, f32[147]{0:T(256)}, u32[]{:S(2)}) copy-start(f32[147]{0:T(256)} %copy-done.38) | copy-start | bytes 1768
  475.1 53.4 %copy-start.43 = (f32[768]{0:T(1024)S(1)}, f32[768]{0:T(1024)}, u32[]{:S(2)}) copy-start(f32[768]{0:T(1024)} %param.30) | copy-start | bytes 9220
  529.8 4.8 copy-start.26
  (34 other events, 78.1 us)
Sparse Core Ops, SparseCore 0:
  11.6 47.5 all-gather.8
  131.9 47.9 all-gather.12
  182.7 45.5 all-gather.10
  299.2 48.7 all-gather.14
  475.2 49.3 all-reduce.12
where the time goes:
time: 553 us; the launch traced here: 543 us
  blocking collectives  216 us (39%)
  waiting for transfers between devices  169 us (31%)
  matrix products  56.3 us (10%)
  local copies, waits for them, and re-layouts  49.3 us (9%)
  other arithmetic  24.9 us (5%)
  between operations  15.7 us (3%)
  starting transfers between devices  11.1 us (2%)
    unnamed x3, blocking collectives  167 us
    all_gather x1, waiting for transfers between devices, shards(): lax.all_gather(mlp_grad.astype(jnp.bfloat16), 'mp', axis=0, tiled=True)  46.9 us
    all_gather x1, waiting for transfers between devices, forward_pass(): rows_one = lax.all_gather(normed_one, 'mp', axis=0, tiled=True)  43 us
    all_gather x1, waiting for transfers between devices, forward_pass(): rows_two = lax.all_gather(normed_two, 'mp', axis=0, tiled=True)  41.1 us
    all_gather x1, waiting for transfers between devices, shards(): lax.all_gather(attn_grad.astype(jnp.bfloat16), 'mp', axis=0, tiled=True)  37.8 us
    psum x1, blocking collectives, shards(): small_grads = lax.psum(small_grads, 'mp')  28.1 us
    unnamed x128, local copies, waits for them, and re-layouts  24.7 us
    psum x1, blocking collectives, shards(): lax.psum(small_grads.astype(jnp.bfloat16), 'dp').astype(jnp.float32)  21.2 us
  transfers between devices with their start and end apart: 9, of which 5 were waited for; matrix products, arithmetic and copies ran while one was open for 6% of the time, Pallas kernels for 0%

commit v1 on v0

v1 whole, which is shorter than its diff:
```python
import functools

import jax
import jax.numpy as jnp
from jax import lax
from jax.experimental import pallas as pl
from jax.experimental.pallas import tpu as pltpu
from jax.sharding import PartitionSpec as P

HEAD = 32
SIDE = 7
LOCAL_SIDE = 3
WIN = 49
SPAN = 2 * SIDE - 1
ENTRIES = SPAN * SPAN
CENTRE = (SIDE - 1) * SPAN + SIDE - 1
SLOTS = 64
TILE = 128
PACK = 4
GROUP = 4
LANES = 256
EPSILON = 1e-05
NEG_FILL = -1000000000.0
GELU_A = 0.7978845608028654
GELU_B = 0.044715
HIGHEST = lax.Precision.HIGHEST
MESH = pl.DeviceIdType.MESH
BF = jnp.bfloat16
F32 = jnp.float32


def dot(left, right, dims, precision=None):
    return lax.dot_general(
        left, right, (dims, ((), ())), preferred_element_type=F32, precision=precision
    )


def dot_nn(left, right, precision=None):
    return dot(left, right, ((1,), (0,)), precision)


def dot_nt(left, right, precision=None):
    return dot(left, right, ((1,), (1,)), precision)


def dot_tn(left, right, precision=None):
    return dot(left, right, ((0,), (0,)), precision)


def iota(shape, axis):
    return lax.broadcasted_iota(jnp.int32, shape, axis)


def one_hot(cond, dtype):
    return jnp.where(cond, 1.0, 0.0).astype(dtype)


def steps_of(values, width, count):
    total = jnp.zeros_like(values)
    for step in range(1, count):
        total = total + jnp.where(values >= step * width, 1, 0)
    return total


def shear(values, shift):
    moved = pltpu.roll(values, shift, axis=1)
    return pltpu.roll(moved, 0, axis=1, stride=1, stride_axis=0)


def split_two(values):
    high = values.astype(BF)
    return high, (values - high.astype(F32)).astype(BF)


def norm_parts(values):
    mean = jnp.mean(values, axis=-1, keepdims=True)
    centre = values - mean
    spread = jnp.mean(centre * centre, axis=-1, keepdims=True)
    scale = lax.rsqrt(spread + EPSILON)
    return centre * scale, scale


def norm_back(grad_normed, normed, scale):
    return scale * (
        grad_normed
        - jnp.mean(grad_normed, axis=-1, keepdims=True)
        - normed * jnp.mean(grad_normed * normed, axis=-1, keepdims=True)
    )


def slot_place(columns, windows, kinds):
    window = steps_of(columns, WIN, windows)
    slot = columns - WIN * window
    kind = jnp.zeros_like(columns)
    for w in range(windows):
        kind = jnp.where(window == w, kinds[w], kind)
    whole = slot + steps_of(slot, SIDE, SIDE)
    corner = slot + (8 - LOCAL_SIDE) * steps_of(slot, LOCAL_SIDE, LOCAL_SIDE)
    rest = slot + (8 * LOCAL_SIDE - LOCAL_SIDE * LOCAL_SIDE)
    local = jnp.where(slot < LOCAL_SIDE * LOCAL_SIDE, corner, rest)
    place = SLOTS * window + jnp.where(kind == 0, whole, local)
    live = jnp.where(kind == 0, WIN, LOCAL_SIDE * LOCAL_SIDE)
    inside = columns < WIN * windows
    return jnp.where(inside, place, -1), inside & (slot < live)


def body(
    dims,
    kind_ref,
    tok_ref,
    og_ref,
    n1g_ref,
    n1b_ref,
    qkvw_ref,
    qvb_ref,
    tab_ref,
    pw_ref,
    pb_ref,
    n2g_ref,
    n2b_ref,
    f1w_ref,
    f1b_ref,
    f2w_ref,
    f2b_ref,
    out_ref,
    tgrad_ref,
    vec_ref,
    qkvg_ref,
    qvg_ref,
    relg_ref,
    projg_ref,
    f1g_ref,
    f1bg_ref,
    f2g_ref,
    wa,
    wf,
    ft,
    sp,
    pk,
    xs,
    x1s,
    n1s,
    gs,
    stats,
    qb,
    fb,
    h1p,
    qs,
    ks,
    vs,
    at,
    pt,
    bias_whole,
    bias_local,
    hg,
    gg,
    ac,
    dp_s,
    ph,
    rc_h,
    rx_h,
    ph2,
    rc_o,
    rx_o,
    gabp,
    dqs,
    dks,
    dvs,
    dbias,
    dh1,
    ga,
    gf,
    rca,
    rxa,
    ry,
    rz,
    fin,
    sg,
    sg_in,
    sg_group,
    sem_ws,
    sem_wr,
    sem_bs,
    sem_br,
    sem_rs,
    sem_rr,
    sem_hs,
    sem_hr,
    sem_as,
    sem_ar,
    sem_ys,
    sem_yr,
    sem_fs,
    sem_fr,
    sem_ss,
    sem_sr,
    sem_gs,
    sem_gr,
):
    n_dp, n_mp, rows, windows, padded, width, block, hidden = dims
    groups = n_dp // GROUP
    places = SLOTS * windows
    z_count = n_mp // 2
    heads_here = block // HEAD
    tiles = width // TILE
    mp = lax.axis_index("mp")
    dp = lax.axis_index("dp")
    z = mp // 2
    y = mp % 2
    base = (dp // GROUP) * GROUP
    mine = dp % GROUP
    x = mine // 2
    c = mine % 2
    core_dl = x * 2 + (1 - c)
    x_dl = (1 - x) * 2 + c
    xc_dl = (1 - x) * 2 + (1 - c)
    to_core = (base + core_dl, mp)
    to_x = (base + x_dl, mp)
    to_y = (dp, z * 2 + (1 - y))

    def z_at(step):
        return (z + step) % z_count

    def to_z(step):
        return (dp, z_at(step) * 2 + y)

    def to_group(step):
        return ((dp + GROUP * step) % n_dp, mp)

    pending = []

    def send(src, dst, s_sem, r_sem, device):
        copy = pltpu.make_async_remote_copy(
            src_ref=src,
            dst_ref=dst,
            send_sem=s_sem,
            recv_sem=r_sem,
            device_id=device,
            device_id_type=MESH,
        )
        copy.start()
        pending.append(copy)
        return copy

    def forget(copy):
        pending[:] = [other for other in pending if other is not copy]

    def sent(copy):
        copy.wait_send()
        forget(copy)

    barrier = pltpu.get_barrier_semaphore()
    peers = [to_core, to_x, to_y]
    peers += [to_z(step) for step in range(1, z_count)]
    peers += [to_group(step) for step in range(1, groups)]
    for peer in peers:
        pl.semaphore_signal(barrier, inc=1, device_id=peer, device_id_type=MESH)

    own = pl.ds(pl.multiple_of(block * mp, 16), block)

    @pl.when(mine < 3)
    def _():
        wa[mine, own, :] = qkvw_ref[jnp.minimum(mine, 2)].T

    @pl.when(mine == 3)
    def _():
        wa[mine, own, :] = pw_ref[...]

    ft[...] = f1w_ref[...].T
    quarter = pl.ds(pl.multiple_of(block * mine, 16), block)
    wf[0, own, :] = ft[quarter, :]
    wf[1, own, :] = f2w_ref[quarter, :]

    pk[...] = jnp.zeros_like(pk)
    pk[0:heads_here, 0:ENTRIES] = tab_ref[...].T
    pk[3:5, 0:block] = qvb_ref[...]
    pk[5:6, :] = f1b_ref[...]
    sp[mp] = pk[...]

    pl.semaphore_wait(barrier, len(peers))

    def rows_of(other_z, other_y):
        return pl.ds(pl.multiple_of(block * (other_z * 2 + other_y), 16), block)

    class Gather:
        def __init__(self, index, buffer, part):
            self.index, self.buffer, self.part = index, buffer, part
            self.along_z, self.along_y = [None], []

        def forward_y(self, part):
            k = len(self.along_y)
            ref = self.buffer.at[part]
            self.along_y.append(
                send(ref, ref, sem_ws.at[self.index, z_count + k], sem_wr.at[self.index, z_count + k], to_y)
            )

        def start(self):
            ref = self.buffer.at[self.part(z, y)]
            for step in range(1, z_count):
                self.along_z.append(
                    send(
                        ref,
                        ref,
                        sem_ws.at[self.index, step - 1],
                        sem_wr.at[self.index, step - 1],
                        to_z(step),
                    )
                )
            self.forward_y(self.part(z, y))

        def arrive_z(self, step):
            self.along_z[step].wait_recv()
            part = self.part((z + z_count - step) % z_count, y)
            self.forward_y(part)
            return part

        def arrive_y(self, step):
            self.along_y[step].wait_recv()
            return self.part((z + z_count - step) % z_count, 1 - y)

    small = Gather(0, sp, lambda oz, oy: oz * 2 + oy)
    attn_w = Gather(1, wa.at[mine], rows_of)
    fc1_w = Gather(2, wf.at[0], rows_of)
    fc2_w = Gather(3, wf.at[1], rows_of)

    small.start()
    attn_w.start()

    def send_rows(ring, index, slot, device, k):
        return send(ring.at[slot], ring.at[slot], sem_rs.at[index, k], sem_rr.at[index, k], device)

    kinds = [kind_ref[mp * windows + w] for w in range(windows)]
    place_row, live_row = slot_place(iota((1, padded), 1), windows, kinds)
    place_col, live_col = slot_place(iota((padded, 1), 0), windows, kinds)
    spread = one_hot(iota((places, padded), 0) == place_row, BF)
    gather = one_hot(iota((padded, places), 1) == place_col, BF)
    row_live = jnp.where(live_col, 1.0, 0.0)

    xs[...] = jnp.zeros_like(xs)
    xs[0:rows, :] = tok_ref[...].astype(F32)
    gs[...] = jnp.zeros_like(gs)
    gs[0:rows, :] = og_ref[...].astype(F32)

    sg[...] = jnp.zeros_like(sg)
    masked = gs[...] * row_live
    sg[5:6, :] = jnp.sum(masked, axis=0, keepdims=True)
    gg[mine] = masked.astype(BF)
    gg_x = send_rows(gg, 0, mine, to_x, 0)
    gg_c0 = send_rows(gg, 0, mine, to_core, 1)

    normed_one, scale_one = norm_parts(xs[...])
    n1s[...] = normed_one
    stats[:, 0:1] = scale_one
    h1 = (normed_one * n1g_ref[...] + n1b_ref[...]).astype(BF)
    h1p[...] = dot_nn(spread, h1).astype(BF)

    for step in range(1, z_count):
        small.arrive_z(step)
    along_x = []

    def forward_x(part):
        k = len(along_x)
        ref = wa.at[mine].at[part]
        along_x.append(send(ref, ref, sem_bs.at[k], sem_br.at[k], to_x))

    forward_x(attn_w.part(z, y))
    for step in range(1, z_count):
        forward_x(attn_w.arrive_z(step))
    fc1_w.start()
    for step in range(z_count):
        small.arrive_y(step)
    for step in range(z_count):
        forward_x(attn_w.arrive_y(step))
    core_a = send(wa.at[mine], wa.at[mine], sem_bs.at[n_mp], sem_br.at[n_mp], to_core)

    lane = iota((1, width), 1)
    owner = steps_of(lane, block, n_mp)
    within = lane - block * owner
    pick_row = iota((n_mp, width), 0) == owner
    spots = iota((hidden, width), 0)

    def spread_row(row, offset):
        picked = dot_nn(sp[:, row, :], one_hot(spots == within + offset, F32), HIGHEST)
        return jnp.sum(jnp.where(pick_row, picked, 0.0), axis=0, keepdims=True)

    qb[0:1, :] = spread_row(3, 0)
    qb[1:2, :] = spread_row(4, 0)
    fb[0:1, :] = spread_row(5, block * mine)

    def table_place(cells, local):
        row, column = cells >> 3, cells & 7
        spot = SPAN * row + column
        if local:
            last = LOCAL_SIDE - 1
            dead = (row > last) | (column > last)
            spot = jnp.where(dead, SPAN * last + last, spot)
        return spot

    cell = iota((1, LANES), 1)
    cell_head, cell_spot = cell >> 6, cell & 63
    source = iota((PACK * TILE, LANES), 0)
    picks = []
    for local in (False, True):
        picks.append(one_hot(source == TILE * cell_head + table_place(cell_spot, local), BF))
    for tile in range(tiles):
        shifted = []
        for k in range(PACK):
            head = tile * PACK + k
            line = sp[head // heads_here, head % heads_here : head % heads_here + 1, 0:LANES]
            line = jnp.broadcast_to(line, (8, LANES))
            shifted.append(
                jnp.concatenate(
                    [
                        shear(line, (SPAN * r - CENTRE) % LANES)[:, 0:TILE]
                        for r in range(8)
                    ],
                    axis=0,
                )
            )
        high, low = split_two(jnp.concatenate(shifted, axis=1))
        bias_whole[tile] = dot_nn(high, picks[0]) + dot_nn(low, picks[0])
        bias_local[tile] = dot_nn(high, picks[1]) + dot_nn(low, picks[1])

    for step in range(1, z_count):
        fc1_w.arrive_z(step)
    fc2_w.start()

    for copy in along_x:
        copy.wait_recv()
    core_b = send(wa.at[x_dl], wa.at[x_dl], sem_bs.at[n_mp + 1], sem_br.at[n_mp + 1], to_core)
    gg_x.wait_recv()
    gg_c1 = send_rows(gg, 0, x_dl, to_core, 2)
    core_a.wait_recv()
    core_b.wait_recv()

    head_lane = iota((PACK * SLOTS, TILE), 1) >> 5
    head_mask = (iota((PACK * SLOTS, TILE), 0) >> 6) == head_lane
    key_place = iota((SLOTS, 1), 0)
    key_row, key_col = key_place >> 3, key_place & 7
    usable = []
    for w in range(windows):
        side = jnp.where(kinds[w] == 0, SIDE, LOCAL_SIDE)
        usable.append((key_row < side) & (key_col < side))

    def four(values):
        return jnp.where(head_mask, jnp.concatenate([values] * PACK, axis=0), 0.0).astype(BF)

    def fold(values):
        picked = jnp.where(head_mask, values, 0.0)
        total = picked[0:SLOTS]
        for k in range(1, PACK):
            total = total + picked[SLOTS * k : SLOTS * (k + 1)]
        return total

    def attend(tile, carry):
        cols = pl.ds(pl.multiple_of(tile * TILE, TILE), TILE)
        normed = h1p[...]
        q_tile = (dot_nt(normed, wa[0, cols, :]) + qb[0:1, cols]) * HEAD ** (-0.5)
        qs[tile] = q_tile.astype(BF)
        ks[tile] = dot_nt(normed, wa[1, cols, :]).astype(BF)
        vs[tile] = (dot_nt(normed, wa[2, cols, :]) + qb[1:2, cols]).astype(BF)
        for w in range(windows):
            part = pl.ds(SLOTS * w, SLOTS)
            scores = dot_nt(ks[tile, part, :], four(qs[tile, part, :].astype(F32)))
            bias = jnp.where(kinds[w] == 0, bias_whole[tile], bias_local[tile])
            scores = jnp.where(usable[w], scores + bias, NEG_FILL)
            raised = jnp.exp(scores - jnp.max(scores, axis=0, keepdims=True))
            probs = raised / jnp.sum(raised, axis=0, keepdims=True)
            pt[tile * windows + w] = probs
            at[tile, part, :] = fold(dot_tn(probs.astype(BF), vs[tile, part, :])).astype(BF)
        return carry

    lax.fori_loop(0, tiles // 2, attend, 0)
    for step in range(z_count):
        fc1_w.arrive_y(step)
    for step in range(1, z_count):
        fc2_w.arrive_z(step)
    lax.fori_loop(tiles // 2, tiles, attend, 0)

    attn = jnp.concatenate(
        [dot_nn(gather, at[tile]).astype(BF) for tile in range(tiles)], axis=1
    )
    x1 = xs[...] + (dot_nn(attn, wa[3]) + pb_ref[...]) * row_live
    x1s[...] = x1
    normed_two, scale_two = norm_parts(x1)
    hg[mine] = (normed_two * n2g_ref[...] + n2b_ref[...]).astype(BF)
    hg_x = send_rows(hg, 1, mine, to_x, 0)
    hg_c0 = send_rows(hg, 1, mine, to_core, 1)

    for step in range(z_count):
        fc2_w.arrive_y(step)

    def slot_rows(slot):
        return pl.ds(pl.multiple_of(padded * slot, 16), padded)

    def mlp(slot):
        pre = dot_nt(hg[slot], wf[0]) + fb[0:1, :]
        square = pre * pre
        bend = jnp.tanh(GELU_A * (pre + GELU_B * (square * pre)))
        ac[slot_rows(slot), :] = (0.5 * pre * (1.0 + bend)).astype(BF)
        slope = 0.5 * (1.0 + bend) + 0.5 * pre * (1.0 - bend * bend) * (
            GELU_A * (1.0 + 3.0 * GELU_B * square)
        )
        dpre = (dot_nt(gg[slot], wf[1]) * slope).astype(BF)
        dp_s[slot_rows(slot), :] = dpre
        ph[slot] = dot_nn(dpre, wf[0]).astype(BF)

    gg_c0.wait_recv()
    hg_c0.wait_recv()
    hg_x.wait_recv()
    hg_c1 = send_rows(hg, 1, x_dl, to_core, 2)
    gg_c1.wait_recv()
    hg_c1.wait_recv()
    mlp(xc_dl)
    ph_c0 = send(ph.at[xc_dl], rc_h.at[0], sem_hs.at[0, 0], sem_hr.at[0, 0], to_core)
    mlp(core_dl)
    ph_c1 = send(ph.at[core_dl], rc_h.at[1], sem_hs.at[0, 1], sem_hr.at[0, 1], to_core)
    mlp(x_dl)
    ph_c0.wait_recv()
    ph2[0] = (ph[x_dl].astype(F32) + rc_h[0].astype(F32)).astype(BF)
    ph_x = send(ph2.at[0], rx_h, sem_hs.at[0, 2], sem_hr.at[0, 2], to_x)
    mlp(mine)

    half_rows = width // 2
    tiles_half = tiles // 2

    def all_rows(ring):
        return ring[...].reshape(GROUP * padded, width)

    def fc1_grad(tile, carry):
        cols = pl.ds(pl.multiple_of(tile * TILE, TILE), TILE)
        left = dp_s[:, cols]
        gf[0, cols, :] = dot_tn(left, all_rows(hg)).astype(BF)
        return carry

    def fc2_grad(tile, carry):
        cols = pl.ds(pl.multiple_of(tile * TILE, TILE), TILE)
        left = ac[:, cols]
        gf[1, cols, :] = dot_tn(left, all_rows(gg)).astype(BF)
        return carry

    sg[pl.ds(8 + mine, 1), :] = jnp.sum(dp_s[...].astype(F32), axis=0, keepdims=True)

    along_y = {}

    def scatter_y(index, source, other_z):
        part = rows_of(other_z, 1 - y)
        along_y[index, other_z] = send(
            source.at[part],
            ry.at[index, other_z],
            sem_ys.at[index, other_z],
            sem_yr.at[index, other_z],
            to_y,
        )

    lax.fori_loop(0, tiles, fc2_grad, 0)
    for other_z in range(z_count):
        scatter_y(2, gf.at[1], other_z)

    ph_c1.wait_recv()
    ph_x.wait_recv()
    dh2 = ph[mine].astype(F32) + rc_h[1].astype(F32) + rx_h[...].astype(F32)
    sg[3:4, :] = jnp.sum(dh2 * normed_two, axis=0, keepdims=True)
    sg[4:5, :] = jnp.sum(dh2, axis=0, keepdims=True)
    dx1 = gs[...] + norm_back(dh2 * n2g_ref[...], normed_two, scale_two)
    gs[...] = dx1
    gab = dx1 * row_live
    sg[2:3, :] = jnp.sum(gab, axis=0, keepdims=True)
    gab = gab.astype(BF)
    gabp[...] = dot_nn(spread, gab).astype(BF)

    lax.fori_loop(0, tiles, fc1_grad, 0)
    for other_z in range(z_count):
        scatter_y(1, gf.at[0], other_z)

    dbias[...] = jnp.zeros_like(dbias)
    dh1[...] = jnp.zeros_like(dh1)

    def attend_back(tile, carry):
        cols = pl.ds(pl.multiple_of(tile * TILE, TILE), TILE)
        dattn = dot_nt(gabp[...], wa[3, cols, :])
        normed = h1p[...]
        total = jnp.zeros((SLOTS, LANES), F32)
        for w in range(windows):
            part = pl.ds(SLOTS * w, SLOTS)
            d_four = four(dattn[SLOTS * w : SLOTS * (w + 1)])
            q_four = four(qs[tile, part, :].astype(F32))
            probs = pt[tile * windows + w]
            dprob = dot_nt(vs[tile, part, :], d_four)
            weighed = probs * dprob
            ds = weighed - probs * jnp.sum(weighed, axis=0, keepdims=True)
            total = total + ds
            dsb = ds.astype(BF)
            dvs[tile, part, :] = dot_nn(probs.astype(BF), d_four).astype(BF)
            dks[tile, part, :] = dot_nn(dsb, q_four).astype(BF)
            dqs[tile, part, :] = (
                fold(dot_tn(dsb, ks[tile, part, :])) * HEAD ** (-0.5)
            ).astype(BF)
        dbias[tile] = total
        for s, grads in enumerate((dqs, dks, dvs)):
            ga[s, cols, :] = dot_tn(grads[tile], normed).astype(BF)
            dh1[...] += dot_nn(grads[tile], wa[s, cols, :])
        sg[6:7, cols] = jnp.sum(dqs[tile].astype(F32), axis=0, keepdims=True)
        sg[7:8, cols] = jnp.sum(dvs[tile].astype(F32), axis=0, keepdims=True)
        attn_tile = dot_nn(gather, at[tile]).astype(BF)
        ga[3, cols, :] = dot_tn(attn_tile, gab).astype(BF)
        return carry

    halves = [pl.ds(0, half_rows), pl.ds(half_rows, half_rows)]
    core_copies, x_copies = [], []

    def reduce_core(half):
        for k, slot in enumerate((xc_dl, core_dl)):
            core_copies.append(
                send(
                    ga.at[slot].at[halves[half]],
                    rca.at[k].at[halves[half]],
                    sem_as.at[half, k],
                    sem_ar.at[half, k],
                    to_core,
                )
            )

    def reduce_x(half):
        part = halves[half]
        core_copies[2 * half].wait_recv()
        rca[0, part, :] = (ga[x_dl, part, :].astype(F32) + rca[0, part, :].astype(F32)).astype(BF)
        x_copies.append(
            send(
                rca.at[0].at[part],
                rxa.at[part],
                sem_as.at[half, 2],
                sem_ar.at[half, 2],
                to_x,
            )
        )

    lax.fori_loop(0, tiles_half, attend_back, 0)
    reduce_core(0)

    def mlp_out(slot):
        ph[slot] = dot_nn(ac[slot_rows(slot), :], wf[1]).astype(BF)

    out_copies = []
    sent(ph_c0)
    sent(ph_c1)
    mlp_out(xc_dl)
    out_copies.append(send(ph.at[xc_dl], rc_o.at[0], sem_hs.at[1, 0], sem_hr.at[1, 0], to_core))
    mlp_out(core_dl)
    out_copies.append(send(ph.at[core_dl], rc_o.at[1], sem_hs.at[1, 1], sem_hr.at[1, 1], to_core))
    reduce_x(0)
    mlp_out(x_dl)
    out_copies[0].wait_recv()
    ph2[1] = (ph[x_dl].astype(F32) + rc_o[0].astype(F32)).astype(BF)
    lax.fori_loop(tiles_half, tiles, attend_back, 0)
    reduce_core(1)
    out_copies.append(send(ph2.at[1], rx_o, sem_hs.at[1, 2], sem_hr.at[1, 2], to_x))
    mlp_out(mine)

    along_z = {}

    def scatter_z(index, source):
        for other_z in range(z_count):
            along_y[index, other_z].wait_recv()
            part = rows_of(other_z, y)
            ry[index, other_z] = (
                ry[index, other_z].astype(F32) + source[part, :].astype(F32)
            ).astype(BF)
        for step in range(1, z_count):
            along_z[index, step] = send(
                ry.at[index, z_at(step)],
                rz.at[index, step - 1],
                sem_fs.at[index, step - 1],
                sem_fr.at[index, step - 1],
                to_z(step),
            )

    scatter_z(2, gf.at[1])
    reduce_x(1)
    scatter_z(1, gf.at[0])

    d_high = dh1[...].astype(BF)
    dh1c = dot_nn(gather, d_high)
    n1 = n1s[...]
    sg[0:1, :] = jnp.sum(dh1c * n1, axis=0, keepdims=True)
    sg[1:2, :] = jnp.sum(dh1c, axis=0, keepdims=True)
    dn = norm_back(dh1c * n1g_ref[...], n1, stats[:, 0:1])
    tgrad_ref[...] = (gs[...] + dn).astype(BF)[0:rows]

    back = one_hot(
        iota((LANES, PACK * TILE), 1)
        == TILE * (iota((LANES, 1), 0) >> 6)
        + (TILE - 1 - table_place(iota((LANES, 1), 0) & 63, False)),
        BF,
    )
    for tile in range(tiles):
        high, low = split_two(dbias[tile])
        wide = dot_nn(high, back) + dot_nn(low, back)
        for k in range(PACK):
            head = tile * PACK + k
            line = jnp.zeros((8, LANES), F32)
            for r in range(8):
                piece = wide[8 * r : 8 * (r + 1), TILE * k : TILE * (k + 1)]
                piece = jnp.concatenate([piece, jnp.zeros_like(piece)], axis=1)
                shift = LANES - 1 - CENTRE - (TILE - 1) + SPAN * r
                line = line + shear(piece, shift)
            row, spot = 12 + head // heads_here, LANES * (head % heads_here)
            sg[row : row + 1, spot : spot + LANES] = jnp.sum(line, axis=0, keepdims=True)

    def small_sum(stage, devices):
        copies = [
            send(
                sg,
                sg_in.at[stage + k],
                sem_ss.at[stage + k],
                sem_sr.at[stage + k],
                device,
            )
            for k, device in enumerate(devices)
        ]
        for copy in copies:
            copy.wait()
            forget(copy)
        total = sg[...]
        for k in range(len(devices)):
            total = total + sg_in[stage + k]
        sg[...] = total

    small_sum(0, [to_core])
    small_sum(1, [to_x])

    out_copies[1].wait_recv()
    out_copies[2].wait_recv()
    branch = ph[mine].astype(F32) + rc_o[1].astype(F32) + rx_o[...].astype(F32)
    out_ref[...] = (x1s[...] + (branch + f2b_ref[...]) * row_live).astype(BF)[0:rows]

    small_sum(2, [to_y])

    for half in range(2):
        part = halves[half]
        core_copies[2 * half + 1].wait_recv()
        x_copies[half].wait_recv()
        ga[mine, part, :] = (
            ga[mine, part, :].astype(F32)
            + rca[1, part, :].astype(F32)
            + rxa[part, :].astype(F32)
        ).astype(BF)
        for other_z in range(half * (z_count // 2), (half + 1) * (z_count // 2)):
            scatter_y(0, ga.at[mine], other_z)

    small_sum(3, [to_z(step) for step in range(1, z_count)])
    if groups > 1:
        small_sum(2 + z_count, [to_group(step) for step in range(1, groups)])

    final_copies = {}

    def finish(index):
        total = ry[index, z].astype(F32)
        for step in range(1, z_count):
            along_z[index, step].wait_recv()
            total = total + rz[index, step - 1].astype(F32)
        fin[index, mine] = total.astype(BF)
        if groups > 1:
            for step in range(1, groups):
                copy = send(
                    fin.at[index, mine],
                    sg_group.at[index, step - 1],
                    sem_gs.at[index, step - 1],
                    sem_gr.at[index, step - 1],
                    to_group(step),
                )
                copy.wait()
                forget(copy)
                total = total + sg_group[index, step - 1].astype(F32)
            fin[index, mine] = total.astype(BF)
        slot = fin.at[index, mine]
        sems = 3 + 3 * index
        final_copies[index, 0] = send(slot, slot, sem_fs.at[3, sems], sem_fr.at[3, sems], to_x)
        final_copies[index, 1] = send(
            slot, slot, sem_fs.at[3, sems + 1], sem_fr.at[3, sems + 1], to_core
        )

    def finish_core(index):
        final_copies[index, 0].wait_recv()
        slot = fin.at[index, x_dl]
        sems = 3 + 3 * index
        final_copies[index, 2] = send(
            slot, slot, sem_fs.at[3, sems + 2], sem_fr.at[3, sems + 2], to_core
        )

    def finish_wait(index):
        final_copies[index, 1].wait_recv()
        final_copies[index, 2].wait_recv()

    finish(2)
    finish(1)
    scatter_z(0, ga.at[mine])
    finish_core(2)
    finish_core(1)
    finish_wait(2)
    f2g_ref[...] = fin[2].reshape(hidden, width).astype(F32)
    finish_wait(1)
    f1g_ref[...] = fin[1].reshape(hidden, width).astype(F32).T

    vec_ref[...] = sg[0:8, :]
    pick = one_hot(iota((width, block), 0) == block * mp + iota((width, block), 1), F32)
    qvg_ref[...] = dot_nn(sg[0:8, :], pick, HIGHEST)[6:8]
    wide_lane = iota((width, hidden), 1)
    pick = one_hot(
        iota((width, hidden), 0) == block * mp + wide_lane - block * steps_of(wide_lane, block, hidden // block), F32
    )
    lines = dot_nn(sg[8:16, :], pick, HIGHEST)
    keep = iota((8, hidden), 0) == steps_of(iota((8, hidden), 1), block, hidden // block)
    f1bg_ref[...] = jnp.sum(jnp.where(keep, lines, 0.0), axis=0, keepdims=True)
    table = sg[pl.ds(12 + mp, 1), :]
    table = jnp.concatenate(
        [table[:, LANES * k : LANES * (k + 1)] for k in range(heads_here)]
        + [jnp.zeros((8 - heads_here, LANES), F32)],
        axis=0,
    )
    turn = one_hot(iota((176, LANES), 0) + iota((176, LANES), 1) == LANES - 1, F32)
    relg_ref[...] = dot_nt(turn, table, HIGHEST)[0:ENTRIES, 0:heads_here]

    finish(0)
    finish_core(0)
    finish_wait(0)
    for s in range(3):
        qkvg_ref[s] = fin[0, s].astype(F32).T
    projg_ref[...] = fin[0, 3].astype(F32)

    for copy in pending:
        copy.wait_send()


def solution(mesh):
    n_dp, n_mp = mesh.shape["dp"], mesh.shape["mp"]

    def shards(
        tokens,
        crop_kind,
        norm1_gain,
        norm1_bias,
        qkv_weight,
        qv_bias,
        rel_table,
        proj_weight,
        proj_bias,
        norm2_gain,
        norm2_bias,
        fc1_weight,
        fc1_bias,
        fc2_weight,
        fc2_bias,
        out_grad,
    ):
        rows, width = tokens.shape
        windows = rows // WIN
        padded = -(-rows // 16) * 16
        block = proj_weight.shape[0]
        hidden = fc2_weight.shape[0]
        heads_here = rel_table.shape[1]
        places = SLOTS * windows
        tiles = width // TILE
        z_count = n_mp // 2
        groups = n_dp // GROUP
        dims = (n_dp, n_mp, rows, windows, padded, width, block, hidden)

        def line(vector):
            return vector.reshape(1, -1)

        def full(*shape):
            return jax.ShapeDtypeStruct(shape, F32)

        vmem = pl.BlockSpec(memory_space=pltpu.VMEM)
        dma = pltpu.SemaphoreType.DMA
        results = pl.pallas_call(
            functools.partial(body, dims),
            out_shape=[
                jax.ShapeDtypeStruct((rows, width), BF),
                jax.ShapeDtypeStruct((rows, width), BF),
                full(8, width),
                full(3, width, block),
                full(2, block),
                full(ENTRIES, heads_here),
                full(block, width),
                full(width, hidden),
                full(1, hidden),
                full(hidden, width),
            ],
            in_specs=[pl.BlockSpec(memory_space=pltpu.SMEM)] + [vmem] * 15,
            out_specs=[vmem] * 10,
            scratch_shapes=[
                pltpu.VMEM((GROUP, width, width), BF),
                pltpu.VMEM((2, width, width), BF),
                pltpu.VMEM((hidden, width), BF),
                pltpu.VMEM((n_mp, 8, hidden), F32),
                pltpu.VMEM((8, hidden), F32),
                pltpu.VMEM((padded, width), F32),
                pltpu.VMEM((padded, width), F32),
                pltpu.VMEM((padded, width), F32),
                pltpu.VMEM((padded, width), F32),
                pltpu.VMEM((padded, TILE), F32),
                pltpu.VMEM((8, width), F32),
                pltpu.VMEM((8, width), F32),
                pltpu.VMEM((places, width), BF),
                pltpu.VMEM((tiles, places, TILE), BF),
                pltpu.VMEM((tiles, places, TILE), BF),
                pltpu.VMEM((tiles, places, TILE), BF),
                pltpu.VMEM((tiles, places, TILE), BF),
                pltpu.VMEM((tiles * windows, SLOTS, LANES), F32),
                pltpu.VMEM((tiles, SLOTS, LANES), F32),
                pltpu.VMEM((tiles, SLOTS, LANES), F32),
                pltpu.VMEM((GROUP, padded, width), BF),
                pltpu.VMEM((GROUP, padded, width), BF),
                pltpu.VMEM((GROUP * padded, width), BF),
                pltpu.VMEM((GROUP * padded, width), BF),
                pltpu.VMEM((GROUP, padded, width), BF),
                pltpu.VMEM((2, padded, width), BF),
                pltpu.VMEM((padded, width), BF),
                pltpu.VMEM((2, padded, width), BF),
                pltpu.VMEM((2, padded, width), BF),
                pltpu.VMEM((padded, width), BF),
                pltpu.VMEM((places, width), BF),
                pltpu.VMEM((tiles, places, TILE), BF),
                pltpu.VMEM((tiles, places, TILE), BF),
                pltpu.VMEM((tiles, places, TILE), BF),
                pltpu.VMEM((tiles, SLOTS, LANES), F32),
                pltpu.VMEM((places, width), F32),
                pltpu.VMEM((GROUP, width, width), BF),
                pltpu.VMEM((2, width, width), BF),
                pltpu.VMEM((2, width, width), BF),
                pltpu.VMEM((width, width), BF),
                pltpu.VMEM((3, z_count, block, width), BF),
                pltpu.VMEM((3, z_count - 1, block, width), BF),
                pltpu.VMEM((3, GROUP, block, width), BF),
                pltpu.VMEM((24, width), F32),
                pltpu.VMEM((2 + z_count + groups, 24, width), F32),
                pltpu.VMEM((3, max(groups - 1, 1), block, width), BF),
                dma((4, 2 * z_count + 2)),
                dma((4, 2 * z_count + 2)),
                dma((n_mp + 2,)),
                dma((n_mp + 2,)),
                dma((2, 3)),
                dma((2, 3)),
                dma((2, 3)),
                dma((2, 3)),
                dma((2, 3)),
                dma((2, 3)),
                dma((3, z_count)),
                dma((3, z_count)),
                dma((4, 12)),
                dma((4, 12)),
                dma((2 + z_count + groups,)),
                dma((2 + z_count + groups,)),
                dma((3, max(groups - 1, 1))),
                dma((3, max(groups - 1, 1))),
            ],
            compiler_params=pltpu.CompilerParams(
                collective_id=0, has_side_effects=True, vmem_limit_bytes=63 * 2**20
            ),
        )(
            crop_kind,
            tokens,
            out_grad,
            line(norm1_gain),
            line(norm1_bias),
            qkv_weight,
            qv_bias,
            rel_table,
            proj_weight,
            line(proj_bias),
            line(norm2_gain),
            line(norm2_bias),
            fc1_weight,
            line(fc1_bias),
            fc2_weight,
            line(fc2_bias),
        )
        block_out, tokens_grad, vec, qkvg, qvg, relg, projg, f1g, f1bg, f2g = results
        return (
            block_out,
            tokens_grad,
            vec[0],
            vec[1],
            qkvg,
            qvg,
            relg,
            projg,
            vec[2],
            vec[3],
            vec[4],
            f1g,
            f1bg.reshape(-1),
            f2g,
            vec[5],
        )

    in_specs = (
        P(("dp", "mp"), None),
        P("dp"),
        P(),
        P(),
        P(None, None, "mp"),
        P(None, "mp"),
        P(None, "mp"),
        P("mp", None),
        P(),
        P(),
        P(),
        P(None, "mp"),
        P("mp"),
        P("mp", None),
        P(),
        P(("dp", "mp"), None),
    )
    out_specs = (
        P(("dp", "mp"), None),
        P(("dp", "mp"), None),
        P(),
        P(),
        P(None, None, "mp"),
        P(None, "mp"),
        P(None, "mp"),
        P("mp", None),
        P(),
        P(),
        P(),
        P(None, "mp"),
        P("mp"),
        P("mp", None),
        P(),
    )
    return jax.shard_map(shards, mesh=mesh, in_specs=in_specs, out_specs=out_specs, check_vma=False)
```

time: 553 us -> 180 us (0.33); the launches traced: 543 us -> 176 us
  blocking collectives: 216 us -> 0 us
  waiting for transfers between devices: 169 us -> 0 us
  Pallas kernels: 0 us -> 150 us
  matrix products: 56.3 us -> 0 us
  local copies, waits for them, and re-layouts: 49.3 us -> 23.5 us
  other arithmetic: 24.9 us -> 1.31 us
  between operations: 15.7 us -> 0.68 us
  starting transfers between devices: 11.1 us -> 0 us
    all_gather x4 -> x0, waiting for transfers between devices: 169 us -> none  [the longest x1 46.9 us: shards(): lax.all_gather(mlp_grad.astype(jnp.bfloat16), 'mp', axis=0, tiled=True)]
    unnamed x3 -> x0, blocking collectives: 167 us -> none
    pallas_call x0 -> x1, Pallas kernels: none -> 150 us  [shards(): pl.pallas_call(functools.partial(body, dims), out_shape=[jax.ShapeDtypeSt...]
    dot_general x26 -> x0, matrix products: 56.3 us -> none  [the longest x6 15.2 us: dot_rows(): lax.dot_general(left, right, (((0,), (0,)), ((), ())), preferred_element_...]
    psum x2 -> x0, blocking collectives: 49.3 us -> none  [the longest x1 28.1 us: shards(): small_grads = lax.psum(small_grads, 'mp')]
    unnamed x128 -> x22, local copies, waits for them, and re-layouts: 24.7 us -> 13.1 us
    unnamed x4 -> x0, starting transfers between devices: 10.5 us -> none
    convert_element_type x10 -> x0, other arithmetic: 9.06 us -> none  [the longest x1 1.99 us: shards(): lax.psum(qkv_weight_grad.astype(jnp.bfloat16), 'dp').astype(jnp.float32)]
  transfers between devices with their start and end apart: 9 -> 0, of which waited for: 5 -> 0; matrix products, arithmetic and copies ran while one was open for 6% -> 0% of each run, Pallas kernels for 0% -> 0%
where the time goes in v1:
time: 180 us; the launch traced here: 176 us
  Pallas kernels  150 us (83%)
  local copies, waits for them, and re-layouts  23.5 us (13%)
    pallas_call x1, Pallas kernels, shards(): pl.pallas_call(functools.partial(body, dims), out_shape=[jax.ShapeDtypeSt...  150 us
    unnamed x22, local copies, waits for them, and re-layouts  13.1 us
    reshape x7, local copies, waits for them, and re-layouts, line(): return vector.reshape(1, -1)  8.84 us

profile of v1, /device:TPU:1, one launch (start us, length us, event | category | flops | bytes accessed | tf_op | source)
XLA Modules:
  0.0 176.0 jit_solution(18061754723111677774)
XLA Ops:
  0.6 1.2 reshape.59.f1b_ref
  1.9 1.3 reshape.54.n1g_ref
  3.2 1.3 reshape.55.n1b_ref
  4.4 1.3 reshape.56.pb_ref
  5.7 1.3 reshape.57.n2g_ref
  7.0 1.3 reshape.58.n2b_ref
  8.2 1.3 reshape.60.f2b_ref
  9.5 1.4 copy.32.tab_ref
  10.9 2.1 %copy.31.qkvw_ref = bf16[3,768,96]{2,1,0:T(8,128)(2,1)} copy(bf16[3,768,96]{1,2,0:T(8,128)(2,1)} %param.20) | data formatting | bytes 884736 | tf_op args[4]
  13.0 150.5 %shard_map.271 = (bf16[147,768]{1,0:T(8,128)(2,1)}, bf16[147,768]{1,0:T(8,128)(2,1)}, f32[8,768]{1,0:T(8,128)}, f32[3,768,96]{2,1,0:T(8,128)}, f32[2,96]{1,0:T(2...) custom-call(s32[24]{0:T(128)} %kind_ref.1, ...), custom_call_target="tpu_custom_call" | custom-call | tf_op jit(solution)/shard_map/pallas_call | solution.py:876
  163.5 0.0 copy-start.4
  163.5 1.3 reduce.5
  164.8 1.6 copy.34
  166.4 1.6 slice_reduce_fusion
  168.0 0.0 copy-start.3
  168.0 0.0 copy-start.5
  168.0 0.0 copy-start.2
  168.0 2.6 %copy.33 = f32[3,768,96]{1,2,0:T(8,128)} copy(f32[3,768,96]{2,1,0:T(8,128)} %get-tuple-element.39) | data formatting | bytes 1769472
  170.6 0.0 copy-done.4
  170.6 0.0 copy-start.1
  170.6 0.7 copy.41
  171.3 0.0 copy-done.3
  171.3 0.7 copy.42
  172.0 0.0 copy-done.5
  172.0 0.6 copy.43
  172.6 0.0 copy-done.2
  172.6 0.7 copy.44
  173.3 0.0 copy-done.1
  173.3 0.0 copy-start
  173.3 1.0 copy.45
  174.3 0.7 copy-done
  175.0 1.0 copy.46
Async XLA Ops:
  163.5 7.1 %copy-start.4 = (bf16[147,768]{1,0:T(8,128)(2,1)S(1)}, bf16[147,768]{1,0:T(8,128)(2,1)}, u32[]{:S(2)}) copy-start(bf16[147,768]{1,0:T(8,128)(2,1)} %get-tuple-element.71) | copy-start | bytes 677380
  168.0 3.3 %copy-start.3 = (bf16[147,768]{1,0:T(8,128)(2,1)S(1)}, bf16[147,768]{1,0:T(8,128)(2,1)}, u32[]{:S(2)}) copy-start(bf16[147,768]{1,0:T(8,128)(2,1)} %get-tuple-element.72) | copy-start | bytes 677380
  168.0 4.0 %copy-start.5 = (f32[2,96]{1,0:T(2,128)S(1)}, f32[2,96]{1,0:T(2,128)}, u32[]{:S(2)}) copy-start(f32[2,96]{1,0:T(2,128)} %get-tuple-element.76) | copy-start | bytes 2308
  168.0 4.6 %copy-start.2 = (f32[96,768]{1,0:T(8,128)S(1)}, f32[96,768]{1,0:T(8,128)}, u32[]{:S(2)}) copy-start(f32[96,768]{1,0:T(8,128)} %get-tuple-element.78) | copy-start | bytes 884740
  170.6 2.7 %copy-start.1 = (f32[768,384]{1,0:T(8,128)S(1)}, f32[768,384]{1,0:T(8,128)}, u32[]{:S(2)}) copy-start(f32[768,384]{1,0:T(8,128)} %get-tuple-element.82) | copy-start | bytes 3538948
  173.3 1.7 copy-start

commit v2 on v1

v2 whole, which is shorter than its diff:
```python
import functools

import jax
import jax.numpy as jnp
from jax import lax
from jax.experimental import pallas as pl
from jax.experimental.pallas import tpu as pltpu
from jax.sharding import PartitionSpec as P

HEAD = 32
SIDE = 7
LOCAL_SIDE = 3
WIN = 49
SPAN = 2 * SIDE - 1
ENTRIES = SPAN * SPAN
CENTRE = (SIDE - 1) * SPAN + SIDE - 1
SLOTS = 64
TILE = 128
PACK = 4
GROUP = 4
LANES = 256
EPSILON = 1e-05
NEG_FILL = -1000000000.0
GELU_A = 0.7978845608028654
GELU_B = 0.044715
HIGHEST = lax.Precision.HIGHEST
MESH = pl.DeviceIdType.MESH
BF = jnp.bfloat16
F32 = jnp.float32


def dot(left, right, dims, precision=None):
    return lax.dot_general(
        left, right, (dims, ((), ())), preferred_element_type=F32, precision=precision
    )


def dot_nn(left, right, precision=None):
    return dot(left, right, ((1,), (0,)), precision)


def dot_nt(left, right, precision=None):
    return dot(left, right, ((1,), (1,)), precision)


def dot_tn(left, right, precision=None):
    return dot(left, right, ((0,), (0,)), precision)


def iota(shape, axis):
    return lax.broadcasted_iota(jnp.int32, shape, axis)


def one_hot(cond, dtype):
    return jnp.where(cond, 1.0, 0.0).astype(dtype)


def steps_of(values, width, count):
    total = jnp.zeros_like(values)
    for step in range(1, count):
        total = total + jnp.where(values >= step * width, 1, 0)
    return total


def shear(values, shift):
    moved = pltpu.roll(values, shift, axis=1)
    return pltpu.roll(moved, 0, axis=1, stride=1, stride_axis=0)


def split_two(values):
    high = values.astype(BF)
    return high, (values - high.astype(F32)).astype(BF)


def flat_row(ref):
    return ref[...].reshape(1, -1)


def norm_parts(values):
    mean = jnp.mean(values, axis=-1, keepdims=True)
    centre = values - mean
    spread = jnp.mean(centre * centre, axis=-1, keepdims=True)
    scale = lax.rsqrt(spread + EPSILON)
    return centre * scale, scale


def norm_back(grad_normed, normed, scale):
    return scale * (
        grad_normed
        - jnp.mean(grad_normed, axis=-1, keepdims=True)
        - normed * jnp.mean(grad_normed * normed, axis=-1, keepdims=True)
    )


def slot_place(columns, windows, kinds):
    window = steps_of(columns, WIN, windows)
    slot = columns - WIN * window
    kind = jnp.zeros_like(columns)
    for w in range(windows):
        kind = jnp.where(window == w, kinds[w], kind)
    whole = slot + steps_of(slot, SIDE, SIDE)
    corner = slot + (8 - LOCAL_SIDE) * steps_of(slot, LOCAL_SIDE, LOCAL_SIDE)
    rest = slot + (8 * LOCAL_SIDE - LOCAL_SIDE * LOCAL_SIDE)
    local = jnp.where(slot < LOCAL_SIDE * LOCAL_SIDE, corner, rest)
    place = SLOTS * window + jnp.where(kind == 0, whole, local)
    live = jnp.where(kind == 0, WIN, LOCAL_SIDE * LOCAL_SIDE)
    inside = columns < WIN * windows
    return jnp.where(inside, place, -1), inside & (slot < live)


def body(
    dims,
    kind_ref,
    tok_ref,
    og_ref,
    n1g_ref,
    n1b_ref,
    qkvw_ref,
    qvb_ref,
    tab_ref,
    pw_ref,
    pb_ref,
    n2g_ref,
    n2b_ref,
    f1w_ref,
    f1b_ref,
    f2w_ref,
    f2b_ref,
    out_ref,
    tgrad_ref,
    vec_ref,
    small_ref,
    fin_ref,
    wa,
    wf,
    ft,
    sp,
    pk,
    xs,
    x1s,
    n1s,
    gs,
    stats,
    qb,
    fb,
    h1p,
    qs,
    ks,
    vs,
    at,
    pt,
    bias_whole,
    bias_local,
    hg,
    gg,
    ac,
    dp_s,
    ph,
    rc_h,
    rx_h,
    ph2,
    rc_o,
    rx_o,
    gabp,
    dqs,
    dks,
    dvs,
    dbias,
    dh1,
    ga,
    gf,
    rca,
    rxa,
    ry_a,
    rz_a,
    ry_m,
    rz_m,
    fin,
    fin_a,
    fin_x,
    group_m,
    group_a,
    sg,
    sg_in,
    sem_ws,
    sem_wr,
    sem_bs,
    sem_br,
    sem_rs,
    sem_rr,
    sem_hs,
    sem_hr,
    sem_as,
    sem_ar,
    sem_ys,
    sem_yr,
    sem_zs,
    sem_zr,
    sem_fs,
    sem_fr,
    sem_ss,
    sem_sr,
    sem_gs,
    sem_gr,
):
    n_dp, n_mp, rows, windows, padded, width, block, hidden = dims
    groups = n_dp // GROUP
    places = SLOTS * windows
    z_count = n_mp // 2
    heads_here = block // HEAD
    tiles = width // TILE
    half_width = width // 2
    mp = lax.axis_index("mp")
    dp = lax.axis_index("dp")
    z = mp // 2
    y = mp % 2
    base = (dp // GROUP) * GROUP
    mine = dp % GROUP
    x = mine // 2
    c = mine % 2
    core_dl = x * 2 + (1 - c)
    x_dl = (1 - x) * 2 + c
    xc_dl = (1 - x) * 2 + (1 - c)
    to_core = (base + core_dl, mp)
    to_x = (base + x_dl, mp)
    to_y = (dp, z * 2 + (1 - y))
    near = 2 * x
    far = 2 - 2 * x

    def z_at(step):
        return (z + step) % z_count

    def to_z(step):
        return (dp, z_at(step) * 2 + y)

    def to_group(step):
        return ((dp + GROUP * step) % n_dp, mp)

    pending = []

    def remote(src, dst, s_sem, r_sem, device):
        return pltpu.make_async_remote_copy(
            src_ref=src,
            dst_ref=dst,
            send_sem=s_sem,
            recv_sem=r_sem,
            device_id=device,
            device_id_type=MESH,
        )

    def send(src, dst, s_sem, r_sem, device, when=None):
        copy = remote(src, dst, s_sem, r_sem, device)
        if when is None:
            copy.start()
        else:
            pl.when(when)(copy.start)
        pending.append((copy, when))
        return copy

    def forget(copy):
        pending[:] = [other for other in pending if other[0] is not copy]

    def sent(copy):
        copy.wait_send()
        forget(copy)

    barrier = pltpu.get_barrier_semaphore()
    peers = [to_core, to_x, to_y]
    peers += [to_z(step) for step in range(1, z_count)]
    peers += [to_group(step) for step in range(1, groups)]
    for peer in peers:
        pl.semaphore_signal(barrier, inc=1, device_id=peer, device_id_type=MESH)

    own = pl.ds(pl.multiple_of(block * mp, 16), block)
    my_cols = pl.ds(pl.multiple_of(half_width * c, TILE), half_width)
    her_cols = pl.ds(pl.multiple_of(half_width * (1 - c), TILE), half_width)
    for s in range(3):
        wa[s, own, my_cols] = qkvw_ref[s, :, my_cols]
    wa[3, own, my_cols] = pw_ref[:, my_cols]

    pk[...] = jnp.zeros_like(pk)
    pk[0:heads_here, 0:ENTRIES] = tab_ref[...]
    pk[3:5, 0:block] = qvb_ref[...]
    pk[5:6, :] = flat_row(f1b_ref)
    sp[mp] = pk[...]

    pl.semaphore_wait(barrier, len(peers))

    def rows_of(other_z, other_y):
        return pl.ds(pl.multiple_of(block * (other_z * 2 + other_y), 16), block)

    relayed = z_count == 4
    if relayed:
        order = [2, jnp.where(z == 0, 3, 1), jnp.where(z == 0, 1, 3)]
    else:
        order = list(range(1, z_count))
    inner = (z == 1) | (z == 2)

    def spread_z(buffer, part, index, first):
        ref = buffer.at[part]
        for step in range(1, z_count):
            far_end = {1: z != 3, 2: None, 3: z != 0}[step] if relayed else None
            k = first + step - 1
            send(ref, ref, sem_ws.at[index, k], sem_wr.at[index, k], to_z(step), far_end)

    def arrived_z(buffer, part_of, index, first, place):
        step = order[place]
        part = part_of((z + z_count - step) % z_count)
        ref = buffer.at[part]
        k = first + step - 1
        remote(ref, ref, sem_ws.at[index, k], sem_wr.at[index, k], to_y).wait_recv()
        if relayed and place == 0:
            last = 2 * (z - 1)
            send(
                ref,
                ref,
                sem_ws.at[index, first + 3],
                sem_wr.at[index, first + last],
                (dp, 3 * (z - 1) * 2 + y),
                inner,
            )
        return part

    class Gather:
        def __init__(self, index, buffer, part):
            self.index, self.buffer, self.part = index, buffer, part

        def forward_y(self, part, step):
            k = z_count + step
            ref = self.buffer.at[part]
            send(ref, ref, sem_ws.at[self.index, k], sem_wr.at[self.index, k], to_y)

        def start_y(self):
            self.forward_y(self.part(z, y), 0)

        def start_z(self):
            spread_z(self.buffer, self.part(z, y), self.index, 0)

        def arrive_z(self, place):
            part = arrived_z(self.buffer, lambda oz: self.part(oz, y), self.index, 0, place)
            self.forward_y(part, order[place])
            return part

        def arrive_y(self, place):
            step = 0 if place == 0 else order[place - 1]
            part = self.part((z + z_count - step) % z_count, 1 - y)
            ref = self.buffer.at[part]
            k = z_count + step
            remote(ref, ref, sem_ws.at[self.index, k], sem_wr.at[self.index, k], to_y).wait_recv()
            return part

    class GatherLong:
        def __init__(self, index, buffer, part):
            self.index, self.buffer, self.part = index, buffer, part

        def pair(self):
            ref = self.buffer.at[self.part(z, y)]
            k = 2 * z_count
            return ref, ref, sem_ws.at[self.index, k], sem_wr.at[self.index, k], to_y

        def start_y(self):
            send(*self.pair())

        def start_z(self):
            spread_z(self.buffer, self.part(z, y), self.index, 0)

        def arrive_y(self):
            remote(*self.pair()).wait_recv()
            spread_z(self.buffer, self.part(z, 1 - y), self.index, z_count)

        def arrive_z(self, place):
            for column in range(2):
                other_y = y if column == 0 else 1 - y
                arrived_z(
                    self.buffer,
                    lambda oz: self.part(oz, other_y),
                    self.index,
                    z_count * column,
                    place,
                )

    def half_block(other_z, other_y):
        return rows_of(other_z, other_y), my_cols

    def whole_block(other_z, other_y):
        return (rows_of(other_z, other_y),)

    def quarter_block(other_z, other_y):
        start = block * (other_z * 2 + other_y) + (block // 2) * x
        return pl.ds(pl.multiple_of(start, 16), block // 2), my_cols

    def left_block(other_z, other_y):
        return rows_of(other_z, other_y), pl.ds(0, half_width)

    def right_block(other_z, other_y):
        return rows_of(other_z, other_y), pl.ds(half_width, half_width)

    small = Gather(0, sp, lambda oz, oy: (oz * 2 + oy,))
    near_w = Gather(1, wa.at[near], half_block)
    key_w = Gather(2, wa.at[1], half_block)
    proj_w = Gather(3, wa.at[3], quarter_block)
    fc1_w = Gather(4, wf.at[0], whole_block)
    fc2_w = Gather(5, wf.at[1], left_block)
    fc2_long = GatherLong(6, wf.at[1], right_block)
    later_z, later_y = range(z_count - 1), range(1, z_count)

    for part in (small, near_w, key_w):
        part.start_z()
        part.start_y()

    def send_rows(ring, index, slot, device, k):
        return send(ring.at[slot], ring.at[slot], sem_rs.at[index, k], sem_rr.at[index, k], device)

    kinds = [kind_ref[mp * windows + w] for w in range(windows)]
    place_row, _ = slot_place(iota((1, padded), 1), windows, kinds)
    place_col, live_col = slot_place(iota((padded, 1), 0), windows, kinds)
    spread = one_hot(iota((places, padded), 0) == place_row, BF)
    gather = one_hot(iota((padded, places), 1) == place_col, BF)
    row_live = jnp.where(live_col, 1.0, 0.0)

    gs[...] = jnp.zeros_like(gs)
    gs[0:rows, :] = og_ref[...].astype(F32)
    sg[...] = jnp.zeros_like(sg)
    masked = gs[...] * row_live
    gg[mine] = masked.astype(BF)
    gg_x = send_rows(gg, 0, mine, to_x, 0)
    gg_c0 = send_rows(gg, 0, mine, to_core, 1)
    sg[5:6, :] = jnp.sum(masked, axis=0, keepdims=True)

    xs[...] = jnp.zeros_like(xs)
    xs[0:rows, :] = tok_ref[...].astype(F32)
    normed_one, scale_one = norm_parts(xs[...])
    n1s[...] = normed_one
    stats[:, 0:1] = scale_one
    h1 = (normed_one * flat_row(n1g_ref) + flat_row(n1b_ref)).astype(BF)
    h1p[...] = dot_nn(spread, h1).astype(BF)

    along_x, proj_x = [], []

    def forward_x(part):
        k = len(along_x)
        ref = wa.at[near].at[part]
        along_x.append(send(ref, ref, sem_bs.at[k], sem_br.at[k], to_x))

    def forward_proj(part):
        k = n_mp + 4 + len(proj_x)
        ref = wa.at[3].at[part]
        proj_x.append(send(ref, ref, sem_bs.at[k], sem_br.at[k], to_x))

    ft[...] = f1w_ref[...].T
    quarter = pl.ds(pl.multiple_of(block * mine, 16), block)
    wf[0, own, :] = ft[quarter, :]
    wf[1, own, :] = f2w_ref[quarter, :]
    fc1_w.start_y()
    for place in later_z:
        small.arrive_z(place)
    forward_x(near_w.arrive_y(0))
    for place in later_z:
        forward_x(near_w.arrive_z(place))
        key_w.arrive_z(place)
        if place == 0:
            fc1_w.start_z()
            proj_w.start_z()
            proj_w.start_y()
    fc2_long.start_y()
    fc2_w.start_y()

    for place in range(z_count):
        small.arrive_y(place)
    lane = iota((1, width), 1)
    owner = steps_of(lane, block, n_mp)
    within = lane - block * owner
    pick_row = iota((n_mp, width), 0) == owner
    spots = iota((hidden, width), 0)

    def spread_row(row, offset):
        picked = dot_nn(sp[:, row, :], one_hot(spots == within + offset, F32), HIGHEST)
        return jnp.sum(jnp.where(pick_row, picked, 0.0), axis=0, keepdims=True)

    qb[0:1, :] = spread_row(3, 0)
    qb[1:2, :] = spread_row(4, 0)
    fb[0:1, :] = spread_row(5, block * mine)

    def table_place(cells, local):
        row, column = cells >> 3, cells & 7
        spot = SPAN * row + column
        if local:
            last = LOCAL_SIDE - 1
            dead = (row > last) | (column > last)
            spot = jnp.where(dead, SPAN * last + last, spot)
        return spot

    cell = iota((1, LANES), 1)
    cell_head, cell_spot = cell >> 6, cell & 63
    source = iota((PACK * TILE, LANES), 0)
    picks = []
    for local in (False, True):
        picks.append(one_hot(source == TILE * cell_head + table_place(cell_spot, local), BF))

    def bias_of(tile):
        shifted = []
        for k in range(PACK):
            head = tile * PACK + k
            line = sp[head // heads_here, head % heads_here : head % heads_here + 1, 0:LANES]
            line = jnp.broadcast_to(line, (8, LANES))
            shifted.append(
                jnp.concatenate(
                    [
                        shear(line, (SPAN * r - CENTRE) % LANES)[:, 0:TILE]
                        for r in range(8)
                    ],
                    axis=0,
                )
            )
        high, low = split_two(jnp.concatenate(shifted, axis=1))
        bias_whole[tile] = dot_nn(high, picks[0]) + dot_nn(low, picks[0])
        bias_local[tile] = dot_nn(high, picks[1]) + dot_nn(low, picks[1])

    for tile in range(tiles // 2):
        bias_of(tile)
    for place in later_y:
        forward_x(near_w.arrive_y(place))
        key_w.arrive_y(place)

    def core_half(index, slot, device_cols):
        ref = wa.at[slot, :, device_cols]
        return send(ref, ref, sem_bs.at[n_mp + index], sem_br.at[n_mp + index], to_core)

    key_w.arrive_y(0)
    core_near = core_half(0, near, my_cols)
    core_key = core_half(1, 1, my_cols)
    for place in later_z:
        fc1_w.arrive_z(place)
        forward_proj(proj_w.arrive_z(place))
        if place == 0:
            fc2_long.start_z()
            fc2_long.arrive_y()
            fc2_w.start_z()
    for tile in range(tiles // 2, tiles):
        bias_of(tile)
    for copy in along_x:
        copy.wait_recv()
    core_far = core_half(2, far, my_cols)
    gg_x.wait_recv()
    gg_c1 = send_rows(gg, 0, x_dl, to_core, 2)
    core_near.wait_recv()
    core_key.wait_recv()
    core_far.wait_recv()

    head_lane = iota((PACK * SLOTS, TILE), 1) >> 5
    head_mask = (iota((PACK * SLOTS, TILE), 0) >> 6) == head_lane
    key_place = iota((SLOTS, 1), 0)
    key_row, key_col = key_place >> 3, key_place & 7
    usable = []
    for w in range(windows):
        side = jnp.where(kinds[w] == 0, SIDE, LOCAL_SIDE)
        usable.append((key_row < side) & (key_col < side))

    def four(values):
        return jnp.where(head_mask, jnp.concatenate([values] * PACK, axis=0), 0.0).astype(BF)

    def fold(values):
        picked = jnp.where(head_mask, values, 0.0)
        total = picked[0:SLOTS]
        for k in range(1, PACK):
            total = total + picked[SLOTS * k : SLOTS * (k + 1)]
        return total

    def attend(tile, carry):
        cols = pl.ds(pl.multiple_of(tile * TILE, TILE), TILE)
        normed = h1p[...]
        q_tile = (dot_nt(normed, wa[0, cols, :]) + qb[0:1, cols]) * HEAD ** (-0.5)
        qs[tile] = q_tile.astype(BF)
        ks[tile] = dot_nt(normed, wa[1, cols, :]).astype(BF)
        vs[tile] = (dot_nt(normed, wa[2, cols, :]) + qb[1:2, cols]).astype(BF)
        for w in range(windows):
            part = pl.ds(SLOTS * w, SLOTS)
            scores = dot_nt(ks[tile, part, :], four(qs[tile, part, :].astype(F32)))
            bias = jnp.where(kinds[w] == 0, bias_whole[tile], bias_local[tile])
            scores = jnp.where(usable[w], scores + bias, NEG_FILL)
            raised = jnp.exp(scores - jnp.max(scores, axis=0, keepdims=True))
            probs = raised / jnp.sum(raised, axis=0, keepdims=True)
            pt[tile * windows + w] = probs
            at[tile, part, :] = fold(dot_tn(probs.astype(BF), vs[tile, part, :])).astype(BF)
        return carry

    third = tiles // 3
    lax.fori_loop(0, third, attend, 0)
    for place in range(z_count):
        forward_proj(proj_w.arrive_y(place))
    lax.fori_loop(third, 2 * third, attend, 0)
    for place in later_z:
        fc2_w.arrive_z(place)
        fc2_long.arrive_z(place)
    for copy in proj_x:
        copy.wait_recv()
    core_proj = core_half(3, 3, my_cols)
    lax.fori_loop(2 * third, tiles, attend, 0)
    core_proj.wait_recv()

    attn = jnp.concatenate(
        [dot_nn(gather, at[tile]).astype(BF) for tile in range(tiles)], axis=1
    )
    x1 = xs[...] + (dot_nn(attn, wa[3]) + flat_row(pb_ref)) * row_live
    x1s[...] = x1
    normed_two, scale_two = norm_parts(x1)
    hg[mine] = (normed_two * flat_row(n2g_ref) + flat_row(n2b_ref)).astype(BF)
    hg_x = send_rows(hg, 1, mine, to_x, 0)
    hg_c0 = send_rows(hg, 1, mine, to_core, 1)

    for place in range(z_count):
        fc1_w.arrive_y(place)
    for place in range(z_count):
        fc2_w.arrive_y(place)

    def slot_rows(slot):
        return pl.ds(pl.multiple_of(padded * slot, 16), padded)

    def mlp(slot):
        pre = dot_nt(hg[slot], wf[0]) + fb[0:1, :]
        square = pre * pre
        bend = jnp.tanh(GELU_A * (pre + GELU_B * (square * pre)))
        ac[slot_rows(slot), :] = (0.5 * pre * (1.0 + bend)).astype(BF)
        slope = 0.5 * (1.0 + bend) + 0.5 * pre * (1.0 - bend * bend) * (
            GELU_A * (1.0 + 3.0 * GELU_B * square)
        )
        dpre = (dot_nt(gg[slot], wf[1]) * slope).astype(BF)
        dp_s[slot_rows(slot), :] = dpre
        ph[slot] = dot_nn(dpre, wf[0]).astype(BF)

    mlp(mine)
    gg_c0.wait_recv()
    hg_c0.wait_recv()
    hg_x.wait_recv()
    hg_c1 = send_rows(hg, 1, x_dl, to_core, 2)
    mlp(core_dl)
    ph_c1 = send(ph.at[core_dl], rc_h.at[1], sem_hs.at[0, 1], sem_hr.at[0, 1], to_core)
    gg_c1.wait_recv()
    hg_c1.wait_recv()
    mlp(xc_dl)
    ph_c0 = send(ph.at[xc_dl], rc_h.at[0], sem_hs.at[0, 0], sem_hr.at[0, 0], to_core)
    mlp(x_dl)
    ph_c0.wait_recv()
    ph2[0] = (ph[x_dl].astype(F32) + rc_h[0].astype(F32)).astype(BF)
    ph_x = send(ph2.at[0], rx_h, sem_hs.at[0, 2], sem_hr.at[0, 2], to_x)

    tiles_half = tiles // 2
    z_half = z_count // 2
    along_y, along_z = {}, {}
    sums = {
        0: (ga.at[near], my_cols, ry_a.at[0], rz_a.at[0]),
        1: (ga.at[1], my_cols, ry_a.at[1], rz_a.at[1]),
        2: (ga.at[3], my_cols, ry_a.at[2], rz_a.at[2]),
        3: (gf.at[0], slice(None), ry_m.at[0], rz_m.at[0]),
        4: (gf.at[1], slice(None), ry_m.at[1], rz_m.at[1]),
    }

    def scatter_y(index, half):
        source, cols, landing, _ = sums[index]
        for other_z in range(half * z_half, (half + 1) * z_half):
            along_y[index, other_z] = send(
                source.at[rows_of(other_z, 1 - y), cols],
                landing.at[other_z],
                sem_ys.at[index, other_z],
                sem_yr.at[index, other_z],
                to_y,
            )

    def scatter_z(index):
        source, cols, landing, far_landing = sums[index]
        for other_z in range(z_count):
            along_y[index, other_z].wait_recv()
            landing[other_z] = (
                landing[other_z].astype(F32) + source[rows_of(other_z, y), cols].astype(F32)
            ).astype(BF)
        for step in range(1, z_count):
            along_z[index, step] = send(
                landing.at[z_at(step)],
                far_landing.at[step - 1],
                sem_zs.at[index, step - 1],
                sem_zr.at[index, step - 1],
                to_z(step),
            )

    def all_rows(ring):
        return ring[...].reshape(GROUP * padded, width)

    def fc1_grad(tile, carry):
        cols = pl.ds(pl.multiple_of(tile * TILE, TILE), TILE)
        gf[0, cols, :] = dot_tn(dp_s[:, cols], all_rows(hg)).astype(BF)
        return carry

    def fc2_grad(tile, carry):
        cols = pl.ds(pl.multiple_of(tile * TILE, TILE), TILE)
        gf[1, cols, :] = dot_tn(ac[:, cols], all_rows(gg)).astype(BF)
        return carry

    lax.fori_loop(0, tiles_half, fc2_grad, 0)
    scatter_y(4, 0)
    lax.fori_loop(tiles_half, tiles, fc2_grad, 0)
    scatter_y(4, 1)
    sg[pl.ds(8 + mine, 1), :] = jnp.sum(dp_s[...].astype(F32), axis=0, keepdims=True)

    ph_c1.wait_recv()
    ph_x.wait_recv()
    dh2 = ph[mine].astype(F32) + rc_h[1].astype(F32) + rx_h[...].astype(F32)
    sg[3:4, :] = jnp.sum(dh2 * normed_two, axis=0, keepdims=True)
    sg[4:5, :] = jnp.sum(dh2, axis=0, keepdims=True)
    dx1 = gs[...] + norm_back(dh2 * flat_row(n2g_ref), normed_two, scale_two)
    gs[...] = dx1
    gab = dx1 * row_live
    sg[2:3, :] = jnp.sum(gab, axis=0, keepdims=True)
    gab = gab.astype(BF)
    gabp[...] = dot_nn(spread, gab).astype(BF)

    dbias[...] = jnp.zeros_like(dbias)
    dh1[...] = jnp.zeros_like(dh1)

    def attend_back(tile, carry):
        cols = pl.ds(pl.multiple_of(tile * TILE, TILE), TILE)
        dattn = dot_nt(gabp[...], wa[3, cols, :])
        normed = h1p[...]
        total = jnp.zeros((SLOTS, LANES), F32)
        for w in range(windows):
            part = pl.ds(SLOTS * w, SLOTS)
            d_four = four(dattn[SLOTS * w : SLOTS * (w + 1)])
            q_four = four(qs[tile, part, :].astype(F32))
            probs = pt[tile * windows + w]
            dprob = dot_nt(vs[tile, part, :], d_four)
            weighed = probs * dprob
            ds = weighed - probs * jnp.sum(weighed, axis=0, keepdims=True)
            total = total + ds
            dsb = ds.astype(BF)
            dvs[tile, part, :] = dot_nn(probs.astype(BF), d_four).astype(BF)
            dks[tile, part, :] = dot_nn(dsb, q_four).astype(BF)
            dqs[tile, part, :] = (
                fold(dot_tn(dsb, ks[tile, part, :])) * HEAD ** (-0.5)
            ).astype(BF)
        dbias[tile] = total
        for s, grads in enumerate((dqs, dks, dvs)):
            ga[s, cols, :] = dot_tn(grads[tile], normed).astype(BF)
            dh1[...] += dot_nn(grads[tile], wa[s, cols, :])
        sg[6:7, cols] = jnp.sum(dqs[tile].astype(F32), axis=0, keepdims=True)
        sg[7:8, cols] = jnp.sum(dvs[tile].astype(F32), axis=0, keepdims=True)
        attn_tile = dot_nn(gather, at[tile]).astype(BF)
        ga[3, cols, :] = dot_tn(attn_tile, gab).astype(BF)
        return carry

    half_rows = width // 2
    halves = [pl.ds(0, half_rows), pl.ds(half_rows, half_rows)]
    core_copies, x_copies = [], []

    def reduce_core(half):
        core_copies.append(
            send(
                ga.at[:, halves[half], her_cols],
                rca.at[:, halves[half], :],
                sem_as.at[half, 0],
                sem_ar.at[half, 0],
                to_core,
            )
        )

    def add_core(slot, part):
        ga[slot, part, my_cols] = (
            ga[slot, part, my_cols].astype(F32) + rca[slot, part, :].astype(F32)
        ).astype(BF)

    def reduce_x(half):
        part = halves[half]
        core_copies[half].wait_recv()
        add_core(far, part)
        x_copies.append(
            send(
                ga.at[far, part, my_cols],
                rxa.at[part],
                sem_as.at[half, 1],
                sem_ar.at[half, 1],
                to_x,
            )
        )
        add_core(3, part)
        scatter_y(2, half)
        add_core(1, part)
        scatter_y(1, half)
        add_core(near, part)

    lax.fori_loop(0, tiles_half, attend_back, 0)
    reduce_core(0)
    lax.fori_loop(0, tiles, fc1_grad, 0)
    scatter_y(3, 0)
    scatter_y(3, 1)
    reduce_x(0)
    scatter_z(4)
    lax.fori_loop(tiles_half, tiles, attend_back, 0)
    reduce_core(1)

    def mlp_out(slot):
        ph[slot] = dot_nn(ac[slot_rows(slot), :], wf[1]).astype(BF)

    out_copies = []
    sent(ph_c0)
    sent(ph_c1)
    mlp_out(xc_dl)
    out_copies.append(send(ph.at[xc_dl], rc_o.at[0], sem_hs.at[1, 0], sem_hr.at[1, 0], to_core))
    mlp_out(core_dl)
    out_copies.append(send(ph.at[core_dl], rc_o.at[1], sem_hs.at[1, 1], sem_hr.at[1, 1], to_core))
    reduce_x(1)
    mlp_out(x_dl)
    out_copies[0].wait_recv()
    ph2[1] = (ph[x_dl].astype(F32) + rc_o[0].astype(F32)).astype(BF)
    out_copies.append(send(ph2.at[1], rx_o, sem_hs.at[1, 2], sem_hr.at[1, 2], to_x))
    mlp_out(mine)

    dh1c = dot_nn(gather, dh1[...].astype(BF))
    n1 = n1s[...]
    sg[0:1, :] = jnp.sum(dh1c * n1, axis=0, keepdims=True)
    sg[1:2, :] = jnp.sum(dh1c, axis=0, keepdims=True)
    dn = norm_back(dh1c * flat_row(n1g_ref), n1, stats[:, 0:1])
    tgrad_ref[...] = (gs[...] + dn).astype(BF)[0:rows]

    back = one_hot(
        iota((LANES, PACK * TILE), 1)
        == TILE * (iota((LANES, 1), 0) >> 6)
        + (TILE - 1 - table_place(iota((LANES, 1), 0) & 63, False)),
        BF,
    )
    for tile in range(tiles):
        high, low = split_two(dbias[tile])
        wide = dot_nn(high, back) + dot_nn(low, back)
        for k in range(PACK):
            head = tile * PACK + k
            line = jnp.zeros((8, LANES), F32)
            for r in range(8):
                piece = wide[8 * r : 8 * (r + 1), TILE * k : TILE * (k + 1)]
                piece = jnp.concatenate([piece, jnp.zeros_like(piece)], axis=1)
                shift = LANES - 1 - CENTRE - (TILE - 1) + SPAN * r
                line = line + shear(piece, shift)
            row, spot = 12 + head // heads_here, LANES * (head % heads_here)
            sg[row : row + 1, spot : spot + LANES] = jnp.sum(line, axis=0, keepdims=True)

    def small_start(stage, devices):
        return stage, [
            send(sg, sg_in.at[stage + k], sem_ss.at[stage + k], sem_sr.at[stage + k], device)
            for k, device in enumerate(devices)
        ]

    def small_end(started):
        stage, copies = started
        for copy in copies:
            copy.wait_recv()
            sent(copy)
        total = sg[...]
        for k in range(len(copies)):
            total = total + sg_in[stage + k]
        sg[...] = total

    smalls = small_start(0, [to_core])

    for half in range(2):
        x_copies[half].wait_recv()
        part = halves[half]
        ga[near, part, my_cols] = (
            ga[near, part, my_cols].astype(F32) + rxa[part, :].astype(F32)
        ).astype(BF)
        scatter_y(0, half)

    small_end(smalls)
    smalls = small_start(1, [to_x])

    out_copies[1].wait_recv()
    out_copies[2].wait_recv()
    branch = ph[mine].astype(F32) + rc_o[1].astype(F32) + rx_o[...].astype(F32)
    out_ref[...] = (x1s[...] + (branch + flat_row(f2b_ref)) * row_live).astype(BF)[0:rows]

    small_end(smalls)
    smalls = small_start(2, [to_y])

    scatter_z(2)
    scatter_z(3)
    small_end(smalls)
    smalls = small_start(3, [to_z(step) for step in range(1, z_count)])
    scatter_z(1)

    def total_z(index):
        landing, far_landing = sums[index][2:]
        total = landing[z].astype(F32)
        for step in range(1, z_count):
            along_z[index, step].wait_recv()
            total = total + far_landing[step - 1].astype(F32)
        return total.astype(BF)

    def swap(ref, dst, index, device):
        return send(ref, dst, sem_fs.at[index], sem_fr.at[index], device)

    def over_groups(ref, landing, index):
        for step in range(1, groups):
            k = index * (groups - 1) + step - 1
            copy = send(ref, landing.at[step - 1], sem_gs.at[k], sem_gr.at[k], to_group(step))
            copy.wait_recv()
            sent(copy)
        if groups > 1:
            total = ref[...].astype(F32)
            for step in range(1, groups):
                total = total + landing[step - 1].astype(F32)
            ref[...] = total.astype(BF)

    final = {}
    for k, index in enumerate((4, 3)):
        fin[1 - k, mine] = total_z(index)
        slot = fin.at[1 - k, mine]
        over_groups(slot, group_m.at[1 - k], k)
        final[index, 0] = swap(slot, slot, 3 * k, to_x)
        final[index, 1] = swap(slot, slot, 3 * k + 1, to_core)
    for k, (index, slot) in enumerate(((2, 3), (1, 1))):
        fin_a[slot, :, my_cols] = total_z(index)
        final[index, 0] = swap(fin_a.at[slot, :, my_cols], fin_x.at[k], 6 + k, to_x)
    scatter_z(0)
    for k, index in enumerate((4, 3)):
        final[index, 0].wait_recv()
        slot = fin.at[1 - k, x_dl]
        final[index, 2] = swap(slot, slot, 3 * k + 2, to_core)
    for index in (4, 3):
        final[index, 1].wait_recv()
        final[index, 2].wait_recv()
    fin_ref[1] = fin[0]
    fin_ref[2] = fin[1]
    for k, (index, slot) in enumerate(((2, 3), (1, 1))):
        final[index, 0].wait_recv()
        sent(final[index, 0])
        fin_a[slot, :, my_cols] = (
            fin_a[slot, :, my_cols].astype(F32) + fin_x[k].astype(F32)
        ).astype(BF)
        over_groups(fin_a.at[slot, :, my_cols], group_a.at[k], 2 + k)

    small_end(smalls)
    if groups > 1:
        small_end(small_start(2 + z_count, [to_group(step) for step in range(1, groups)]))

    vec_ref[...] = sg[0:8, :]
    pick = one_hot(iota((width, block), 0) == block * mp + iota((width, block), 1), F32)
    small_ref[0:8, 0:block] = dot_nn(sg[0:8, :], pick, HIGHEST)
    wide_lane = iota((width, hidden), 1)
    pick = one_hot(
        iota((width, hidden), 0)
        == block * mp + wide_lane - block * steps_of(wide_lane, block, hidden // block),
        F32,
    )
    lines = dot_nn(sg[8:16, :], pick, HIGHEST)
    keep = iota((8, hidden), 0) == steps_of(iota((8, hidden), 1), block, hidden // block)
    small_ref[8:9, :] = jnp.sum(jnp.where(keep, lines, 0.0), axis=0, keepdims=True)
    table = sg[pl.ds(12 + mp, 1), :]
    table = jnp.concatenate(
        [table[:, LANES * k : LANES * (k + 1)] for k in range(heads_here)]
        + [jnp.zeros((8 - heads_here, LANES), F32)],
        axis=0,
    )
    turn = one_hot(iota((LANES, LANES), 0) + iota((LANES, LANES), 1) == LANES - 1, F32)
    small_ref[16:24, 0:LANES] = dot_nn(table, turn, HIGHEST)

    fin_a[near, :, my_cols] = total_z(0)
    slot = fin_a.at[near, :, my_cols]
    over_groups(slot, group_a.at[2], 4)
    near_x = swap(slot, slot, 8, to_x)
    near_x.wait_recv()
    slots = fin_a.at[:, :, my_cols]
    swap(slots, slots, 9, to_core).wait_recv()
    fin_ref[0] = fin_a[...]

    for copy, when in pending:
        if when is None:
            copy.wait_send()
        else:
            pl.when(when)(copy.wait_send)


def unpack(
    out_in,
    tgrad_in,
    vec_in,
    small_in,
    fin_in,
    out_ref,
    tgrad_ref,
    n1g_ref,
    n1b_ref,
    qkvg_ref,
    qvg_ref,
    relg_ref,
    projg_ref,
    pbg_ref,
    n2g_ref,
    n2b_ref,
    f1g_ref,
    f1bg_ref,
    f2g_ref,
    f2bg_ref,
):
    hidden, width = f2g_ref.shape
    out_ref[...] = out_in[...]
    tgrad_ref[...] = tgrad_in[...]
    for k, ref in enumerate((n1g_ref, n1b_ref, pbg_ref, n2g_ref, n2b_ref, f2bg_ref)):
        ref[...] = vec_in[k : k + 1, :].reshape(width)
    for s in range(3):
        qkvg_ref[s] = fin_in[0, s].astype(F32)
    projg_ref[...] = fin_in[0, 3].astype(F32)
    f1g_ref[...] = fin_in[1].reshape(hidden, width).astype(F32).T
    f2g_ref[...] = fin_in[2].reshape(hidden, width).astype(F32)
    qvg_ref[...] = small_in[6:8, 0 : qvg_ref.shape[1]]
    f1bg_ref[...] = small_in[8:9, :].reshape(hidden)
    relg_ref[...] = small_in[16 : 16 + relg_ref.shape[0], 0:ENTRIES]


def solution(mesh):
    n_dp, n_mp = mesh.shape["dp"], mesh.shape["mp"]

    def shards(
        tokens,
        crop_kind,
        norm1_gain,
        norm1_bias,
        qkv_weight,
        qv_bias,
        rel_table,
        proj_weight,
        proj_bias,
        norm2_gain,
        norm2_bias,
        fc1_weight,
        fc1_bias,
        fc2_weight,
        fc2_bias,
        out_grad,
    ):
        rows, width = tokens.shape
        windows = rows // WIN
        padded = -(-rows // 16) * 16
        block = proj_weight.shape[0]
        hidden = fc2_weight.shape[0]
        heads_here = rel_table.shape[1]
        places = SLOTS * windows
        tiles = width // TILE
        z_count = n_mp // 2
        groups = n_dp // GROUP
        dims = (n_dp, n_mp, rows, windows, padded, width, block, hidden)

        def full(*shape):
            return jax.ShapeDtypeStruct(shape, F32)

        vmem = pl.BlockSpec(memory_space=pltpu.VMEM)
        dma = pltpu.SemaphoreType.DMA
        results = pl.pallas_call(
            functools.partial(body, dims),
            out_shape=[
                jax.ShapeDtypeStruct((rows, width), BF),
                jax.ShapeDtypeStruct((rows, width), BF),
                full(8, width),
                full(24, hidden),
                jax.ShapeDtypeStruct((3, GROUP, block, width), BF),
            ],
            in_specs=[pl.BlockSpec(memory_space=pltpu.SMEM)] + [vmem] * 15,
            out_specs=[vmem] * 5,
            scratch_shapes=[
                pltpu.VMEM((GROUP, width, width), BF),
                pltpu.VMEM((2, width, width), BF),
                pltpu.VMEM((hidden, width), BF),
                pltpu.VMEM((n_mp, 8, hidden), F32),
                pltpu.VMEM((8, hidden), F32),
                pltpu.VMEM((padded, width), F32),
                pltpu.VMEM((padded, width), F32),
                pltpu.VMEM((padded, width), F32),
                pltpu.VMEM((padded, width), F32),
                pltpu.VMEM((padded, TILE), F32),
                pltpu.VMEM((8, width), F32),
                pltpu.VMEM((8, width), F32),
                pltpu.VMEM((places, width), BF),
                pltpu.VMEM((tiles, places, TILE), BF),
                pltpu.VMEM((tiles, places, TILE), BF),
                pltpu.VMEM((tiles, places, TILE), BF),
                pltpu.VMEM((tiles, places, TILE), BF),
                pltpu.VMEM((tiles * windows, SLOTS, LANES), F32),
                pltpu.VMEM((tiles, SLOTS, LANES), F32),
                pltpu.VMEM((tiles, SLOTS, LANES), F32),
                pltpu.VMEM((GROUP, padded, width), BF),
                pltpu.VMEM((GROUP, padded, width), BF),
                pltpu.VMEM((GROUP * padded, width), BF),
                pltpu.VMEM((GROUP * padded, width), BF),
                pltpu.VMEM((GROUP, padded, width), BF),
                pltpu.VMEM((2, padded, width), BF),
                pltpu.VMEM((padded, width), BF),
                pltpu.VMEM((2, padded, width), BF),
                pltpu.VMEM((2, padded, width), BF),
                pltpu.VMEM((padded, width), BF),
                pltpu.VMEM((places, width), BF),
                pltpu.VMEM((tiles, places, TILE), BF),
                pltpu.VMEM((tiles, places, TILE), BF),
                pltpu.VMEM((tiles, places, TILE), BF),
                pltpu.VMEM((tiles, SLOTS, LANES), F32),
                pltpu.VMEM((places, width), F32),
                pltpu.VMEM((GROUP, width, width), BF),
                pltpu.VMEM((2, width, width), BF),
                pltpu.VMEM((GROUP, width, width // 2), BF),
                pltpu.VMEM((width, width // 2), BF),
                pltpu.VMEM((3, z_count, block, width // 2), BF),
                pltpu.VMEM((3, z_count - 1, block, width // 2), BF),
                pltpu.VMEM((2, z_count, block, width), BF),
                pltpu.VMEM((2, z_count - 1, block, width), BF),
                pltpu.VMEM((2, GROUP, block, width), BF),
                pltpu.VMEM((GROUP, block, width), BF),
                pltpu.VMEM((2, block, width // 2), BF),
                pltpu.VMEM((2, max(groups - 1, 1), block, width), BF),
                pltpu.VMEM((3, max(groups - 1, 1), block, width // 2), BF),
                pltpu.VMEM((24, width), F32),
                pltpu.VMEM((2 + z_count + groups, 24, width), F32),
                dma((7, 2 * z_count + 1)),
                dma((7, 2 * z_count + 1)),
                dma((2 * n_mp + 4,)),
                dma((2 * n_mp + 4,)),
                dma((2, 3)),
                dma((2, 3)),
                dma((2, 3)),
                dma((2, 3)),
                dma((2, 2)),
                dma((2, 2)),
                dma((5, z_count)),
                dma((5, z_count)),
                dma((5, z_count)),
                dma((5, z_count)),
                dma((10,)),
                dma((10,)),
                dma((2 + z_count + groups,)),
                dma((2 + z_count + groups,)),
                dma((5 * max(groups - 1, 1),)),
                dma((5 * max(groups - 1, 1),)),
            ],
            compiler_params=pltpu.CompilerParams(
                collective_id=0, has_side_effects=True, vmem_limit_bytes=63 * 2**20
            ),
        )(
            crop_kind,
            tokens,
            out_grad,
            norm1_gain,
            norm1_bias,
            jnp.swapaxes(qkv_weight, 1, 2),
            qv_bias,
            rel_table.T,
            proj_weight,
            proj_bias,
            norm2_gain,
            norm2_bias,
            fc1_weight,
            fc1_bias,
            fc2_weight,
            fc2_bias,
        )
        results = pl.pallas_call(
            unpack,
            out_shape=[
                jax.ShapeDtypeStruct((rows, width), BF),
                jax.ShapeDtypeStruct((rows, width), BF),
                full(width),
                full(width),
                full(3, block, width),
                full(2, block),
                full(heads_here, ENTRIES),
                full(block, width),
                full(width),
                full(width),
                full(width),
                full(width, hidden),
                full(hidden),
                full(hidden, width),
                full(width),
            ],
            in_specs=[vmem] * 5,
            out_specs=[vmem] * 15,
        )(*results)
        results = list(results)
        results[4] = jnp.swapaxes(results[4], 1, 2)
        results[6] = results[6].T
        return tuple(results)

    in_specs = (
        P(("dp", "mp"), None),
        P("dp"),
        P(),
        P(),
        P(None, None, "mp"),
        P(None, "mp"),
        P(None, "mp"),
        P("mp", None),
        P(),
        P(),
        P(),
        P(None, "mp"),
        P("mp"),
        P("mp", None),
        P(),
        P(("dp", "mp"), None),
    )
    out_specs = (
        P(("dp", "mp"), None),
        P(("dp", "mp"), None),
        P(),
        P(),
        P(None, None, "mp"),
        P(None, "mp"),
        P(None, "mp"),
        P("mp", None),
        P(),
        P(),
        P(),
        P(None, "mp"),
        P("mp"),
        P("mp", None),
        P(),
    )
    return jax.shard_map(shards, mesh=mesh, in_specs=in_specs, out_specs=out_specs, check_vma=False)
```

time: 180 us -> 155 us (0.86); the launches traced: 176 us -> 155 us
  local copies, waits for them, and re-layouts: 23.5 us -> 0 us
  Pallas kernels: 150 us -> 154 us
    unnamed x22 -> x0, local copies, waits for them, and re-layouts: 13.1 us -> none
    reshape x7 -> x0, local copies, waits for them, and re-layouts: 8.84 us -> none  [line(): return vector.reshape(1, -1)]
    pallas_call x0 -> x1, Pallas kernels: none -> 3.9 us  [shards(): pl.pallas_call(unpack, out_shape=[jax.ShapeDtypeStruct((rows, width), BF)...]
where the time goes in v2:
time: 155 us
  Pallas kernels  154 us (99%)
    pallas_call x1, Pallas kernels, shards(): pl.pallas_call(functools.partial(body, dims), out_shape=[jax.ShapeDtypeSt...  150 us
    pallas_call x1, Pallas kernels, shards(): pl.pallas_call(unpack, out_shape=[jax.ShapeDtypeStruct((rows, width), BF)...  3.9 us

profile of v2, /device:TPU:1, one launch (start us, length us, event | category | flops | bytes accessed | tf_op | source)
XLA Modules:
  0.0 154.6 jit_solution(9784195997959542275)
XLA Ops:
  0.7 149.9 %shard_map.271 = (bf16[147,768]{1,0:T(8,128)(2,1)}, bf16[147,768]{1,0:T(8,128)(2,1)}, f32[8,768]{1,0:T(8,128)}, f32[24,384]{1,0:T(8,128)}, bf16[3,4,96,768]{3,2,1,0:T(8,128)(2,1)}) custom-call(s32[24]{0:T(128)} %kind_ref.1, bf16[147,768]{1,0:T(8,128)(2,1)} %tok_ref.1, bf16[147,768]{1,0:T(8,128)(2,1)} %og_ref.1, f32[768]{0:T(1024)} %n1g_ref.1, f32[768]{0:T(1024)} %n1b_ref.1, ...), custom_call_target="tpu_custom_call" | custom-call | tf_op jit(solution)/shard_map/pallas_call | solution.py:1052
  150.5 3.9 %shard_map.272 = (bf16[147,768]{1,0:T(8,128)(2,1)}, bf16[147,768]{1,0:T(8,128)(2,1)}, f32[768]{0:T(1024)}, f32[768]{0:T(1024)}, f32[3,96,768]{2,1,0:T(8,128)}, /...) custom-call(bf16[147,768]{1,0:T(8,128)(2,1)} %get-tuple-element.35.o, ...), custom_call_target="tpu_custom_call" | custom-call | tf_op jit(solution)/shard_map/pallas_call | solution.py:1157

commit v3 on v2

--- a/solution.py
+++ b/solution.py
@@ -171,10 +171,9 @@
     gf,
     rca,
     rxa,
-    ry_a,
-    rz_a,
-    ry_m,
-    rz_m,
+    ry,
+    rz,
+    rr,
     fin,
     fin_a,
     fin_x,
@@ -404,9 +403,13 @@
     fc2_long = GatherLong(6, wf.at[1], right_block)
     later_z, later_y = range(z_count - 1), range(1, z_count)
 
-    for part in (small, near_w, key_w):
+    for part in (near_w, key_w, proj_w, small):
         part.start_z()
         part.start_y()
+    ft[...] = f1w_ref[...].T
+    quarter = pl.ds(pl.multiple_of(block * mine, 16), block)
+    wf[0, own, :] = ft[quarter, :]
+    wf[1, own, :] = f2w_ref[quarter, :]
 
     def send_rows(ring, index, slot, device, k):
         return send(ring.at[slot], ring.at[slot], sem_rs.at[index, k], sem_rr.at[index, k], device)
@@ -423,7 +426,6 @@
     sg[...] = jnp.zeros_like(sg)
     masked = gs[...] * row_live
     gg[mine] = masked.astype(BF)
-    gg_x = send_rows(gg, 0, mine, to_x, 0)
     gg_c0 = send_rows(gg, 0, mine, to_core, 1)
     sg[5:6, :] = jnp.sum(masked, axis=0, keepdims=True)
 
@@ -447,24 +449,38 @@
         ref = wa.at[3].at[part]
         proj_x.append(send(ref, ref, sem_bs.at[k], sem_br.at[k], to_x))
 
-    ft[...] = f1w_ref[...].T
-    quarter = pl.ds(pl.multiple_of(block * mine, 16), block)
-    wf[0, own, :] = ft[quarter, :]
-    wf[1, own, :] = f2w_ref[quarter, :]
-    fc1_w.start_y()
+    forward_x(near_w.arrive_y(0))
+
+    def core_half(index, slot):
+        ref = wa.at[slot, :, my_cols]
+        return send(ref, ref, sem_bs.at[n_mp + index], sem_br.at[n_mp + index], to_core)
+
+    forward_x(near_w.arrive_z(0))
+    fc1_w.start_z()
+    for place in later_z[1:]:
+        forward_x(near_w.arrive_z(place))
+    for place in later_z:
+        key_w.arrive_z(place)
+        forward_proj(proj_w.arrive_z(place))
+    for part in (fc1_w, fc2_w, fc2_long):
+        part.start_y()
     for place in later_z:
         small.arrive_z(place)
-    forward_x(near_w.arrive_y(0))
-    for place in later_z:
-        forward_x(near_w.arrive_z(place))
-        key_w.arrive_z(place)
-        if place == 0:
-            fc1_w.start_z()
-            proj_w.start_z()
-            proj_w.start_y()
-    fc2_long.start_y()
-    fc2_w.start_y()
-
+    for place in later_y:
+        forward_x(near_w.arrive_y(place))
+    fc1_w.arrive_z(0)
+    fc2_w.start_z()
+    for place in range(z_count):
+        forward_proj(proj_w.arrive_y(place))
+    gg_x = send_rows(gg, 0, mine, to_x, 0)
+    for place in later_z[1:]:
+        fc1_w.arrive_z(place)
+    fc2_long.arrive_y()
+    fc2_long.start_z()
+    for place in range(z_count):
+        key_w.arrive_y(place)
+    core_near = core_half(0, near)
+    core_key = core_half(1, 1)
     for place in range(z_count):
         small.arrive_y(place)
     lane = iota((1, width), 1)
@@ -516,33 +532,11 @@
         bias_whole[tile] = dot_nn(high, picks[0]) + dot_nn(low, picks[0])
         bias_local[tile] = dot_nn(high, picks[1]) + dot_nn(low, picks[1])
 
-    for tile in range(tiles // 2):
-        bias_of(tile)
-    for place in later_y:
-        forward_x(near_w.arrive_y(place))
-        key_w.arrive_y(place)
-
-    def core_half(index, slot, device_cols):
-        ref = wa.at[slot, :, device_cols]
-        return send(ref, ref, sem_bs.at[n_mp + index], sem_br.at[n_mp + index], to_core)
-
-    key_w.arrive_y(0)
-    core_near = core_half(0, near, my_cols)
-    core_key = core_half(1, 1, my_cols)
-    for place in later_z:
-        fc1_w.arrive_z(place)
-        forward_proj(proj_w.arrive_z(place))
-        if place == 0:
-            fc2_long.start_z()
-            fc2_long.arrive_y()
-            fc2_w.start_z()
-    for tile in range(tiles // 2, tiles):
+    for tile in range(tiles):
         bias_of(tile)
     for copy in along_x:
         copy.wait_recv()
-    core_far = core_half(2, far, my_cols)
-    gg_x.wait_recv()
-    gg_c1 = send_rows(gg, 0, x_dl, to_core, 2)
+    core_far = core_half(2, far)
     core_near.wait_recv()
     core_key.wait_recv()
     core_far.wait_recv()
@@ -586,15 +580,14 @@
 
     third = tiles // 3
     lax.fori_loop(0, third, attend, 0)
-    for place in range(z_count):
-        forward_proj(proj_w.arrive_y(place))
-    lax.fori_loop(third, 2 * third, attend, 0)
     for place in later_z:
         fc2_w.arrive_z(place)
-        fc2_long.arrive_z(place)
+    gg_x.wait_recv()
+    gg_c1 = send_rows(gg, 0, x_dl, to_core, 2)
+    lax.fori_loop(third, 2 * third, attend, 0)
     for copy in proj_x:
         copy.wait_recv()
-    core_proj = core_half(3, 3, my_cols)
+    core_proj = core_half(3, 3)
     lax.fori_loop(2 * third, tiles, attend, 0)
     core_proj.wait_recv()
 
@@ -608,6 +601,8 @@
     hg_x = send_rows(hg, 1, mine, to_x, 0)
     hg_c0 = send_rows(hg, 1, mine, to_core, 1)
 
+    for place in later_z:
+        fc2_long.arrive_z(place)
     for place in range(z_count):
         fc1_w.arrive_y(place)
     for place in range(z_count):
@@ -646,41 +641,151 @@
 
     tiles_half = tiles // 2
     z_half = z_count // 2
-    along_y, along_z = {}, {}
-    sums = {
-        0: (ga.at[near], my_cols, ry_a.at[0], rz_a.at[0]),
-        1: (ga.at[1], my_cols, ry_a.at[1], rz_a.at[1]),
-        2: (ga.at[3], my_cols, ry_a.at[2], rz_a.at[2]),
-        3: (gf.at[0], slice(None), ry_m.at[0], rz_m.at[0]),
-        4: (gf.at[1], slice(None), ry_m.at[1], rz_m.at[1]),
-    }
-
-    def scatter_y(index, half):
-        source, cols, landing, _ = sums[index]
-        for other_z in range(half * z_half, (half + 1) * z_half):
-            along_y[index, other_z] = send(
-                source.at[rows_of(other_z, 1 - y), cols],
-                landing.at[other_z],
-                sem_ys.at[index, other_z],
-                sem_yr.at[index, other_z],
+
+    def add_to(ref, *others):
+        total = ref[...].astype(F32)
+        for other in others:
+            total = total + other[...].astype(F32)
+        ref[...] = total.astype(BF)
+
+    class Line:
+        def __init__(self, index, part, relay):
+            self.index, self.part = index, part
+            self.relay = relay and relayed
+
+        def recv(self, step):
+            return rz.at[self.index, step - 1]
+
+        def sems(self, k, r):
+            return sem_zs.at[self.index, k], sem_zr.at[self.index, r]
+
+        def over(self):
+            return remote(
+                self.part(z_count - 1 - z),
+                rr.at[self.index],
+                *self.sems(3, 3),
+                (dp, (1 + z // 3) * 2 + y),
+            )
+
+        def far(self):
+            return remote(self.part(z_at(2)), self.recv(2), *self.sems(1, 1), to_z(2))
+
+        def start(self):
+            if not self.relay:
+                for step in range(1, z_count):
+                    send(
+                        self.part(z_at(step)),
+                        self.recv(step),
+                        *self.sems(step - 1, step - 1),
+                        to_z(step),
+                    )
+                return
+            outer = jnp.logical_not(inner)
+            copy = self.over()
+            pl.when(outer)(copy.start)
+            pending.append((copy, outer))
+            for step, when in ((1, z != 3), (3, z != 0)):
+                send(
+                    self.part(z_at(step)),
+                    self.recv(step),
+                    *self.sems(step - 1, step - 1),
+                    to_z(step),
+                    when,
+                )
+            pl.when(outer)(self.far().start)
+
+        def middle(self):
+            if self.relay:
+
+                @pl.when(inner)
+                def _():
+                    self.over().wait_recv()
+                    add_to(self.part(z_at(2)), rr.at[self.index])
+                    self.far().start()
+
+                pending.append((self.far(), None))
+
+        def total(self):
+            whens = [z != 0, None, z != z_count - 1] if self.relay else [None] * (z_count - 1)
+            ref = self.part(z)
+            for step in range(1, z_count):
+                copy = remote(ref, self.recv(step), *self.sems(step - 1, step - 1), to_y)
+
+                def take(copy=copy, step=step):
+                    copy.wait_recv()
+                    add_to(ref, self.recv(step))
+
+                if whens[step - 1] is None:
+                    take()
+                else:
+                    pl.when(whens[step - 1])(take)
+            return ref
+
+    class YFirst:
+        def __init__(self, index, source, cols, relay):
+            self.index, self.source, self.cols = index, source, cols
+            self.line = Line(index, lambda oz: ry.at[index, oz], relay)
+            self.along_y = {}
+
+        def scatter(self, half):
+            for oz in range(half * z_half, (half + 1) * z_half):
+                self.along_y[oz] = send(
+                    self.source.at[rows_of(oz, 1 - y), self.cols],
+                    ry.at[self.index, oz],
+                    sem_ys.at[self.index, oz],
+                    sem_yr.at[self.index, oz],
+                    to_y,
+                )
+
+        def start_z(self):
+            for oz in range(z_count):
+                self.along_y[oz].wait_recv()
+                add_to(ry.at[self.index, oz], self.source.at[rows_of(oz, y), self.cols])
+            self.line.start()
+
+        def middle(self):
+            self.line.middle()
+
+        def total(self):
+            return self.line.total()
+
+    class ZFirst:
+        def __init__(self, index, source, cols):
+            self.index = index
+            self.lines = [
+                Line(index + k, lambda oz, oy=oy: source.at[rows_of(oz, oy), cols], True)
+                for k, oy in enumerate((1 - y, y))
+            ]
+
+        def start_z(self):
+            for line in self.lines:
+                line.start()
+
+        def middle(self):
+            for line in self.lines:
+                line.middle()
+
+        def start_y(self):
+            self.copy = send(
+                self.lines[0].total(),
+                ry.at[self.index, 0],
+                sem_ys.at[self.index, 0],
+                sem_yr.at[self.index, 0],
                 to_y,
             )
 
-    def scatter_z(index):
-        source, cols, landing, far_landing = sums[index]
-        for other_z in range(z_count):
-            along_y[index, other_z].wait_recv()
-            landing[other_z] = (
-                landing[other_z].astype(F32) + source[rows_of(other_z, y), cols].astype(F32)
-            ).astype(BF)
-        for step in range(1, z_count):
-            along_z[index, step] = send(
-                landing.at[z_at(step)],
-                far_landing.at[step - 1],
-                sem_zs.at[index, step - 1],
-                sem_zr.at[index, step - 1],
-                to_z(step),
-            )
+        def total(self):
+            ref = self.lines[1].total()
+            self.copy.wait_recv()
+            add_to(ref, ry.at[self.index, 0])
+            return ref
+
+    left_cols, right_cols = pl.ds(0, half_width), pl.ds(half_width, half_width)
+    sum_near = YFirst(0, ga.at[near], my_cols, False)
+    sum_key = YFirst(1, ga.at[1], my_cols, True)
+    sum_proj = YFirst(2, ga.at[3], my_cols, True)
+    sum_fc1 = [YFirst(3, gf.at[0], left_cols, True), YFirst(4, gf.at[0], right_cols, True)]
+    sum_fc2 = [YFirst(5, gf.at[1], left_cols, True), ZFirst(6, gf.at[1], right_cols)]
 
     def all_rows(ring):
         return ring[...].reshape(GROUP * padded, width)
@@ -696,9 +801,16 @@
         return carry
 
     lax.fori_loop(0, tiles_half, fc2_grad, 0)
-    scatter_y(4, 0)
+    sum_fc2[0].scatter(0)
     lax.fori_loop(tiles_half, tiles, fc2_grad, 0)
-    scatter_y(4, 1)
+    sum_fc2[1].start_z()
+    sum_fc2[0].scatter(1)
+    lax.fori_loop(0, tiles_half, fc1_grad, 0)
+    for part in sum_fc1:
+        part.scatter(0)
+    lax.fori_loop(tiles_half, tiles, fc1_grad, 0)
+    for part in sum_fc1:
+        part.scatter(1)
     sg[pl.ds(8 + mine, 1), :] = jnp.sum(dp_s[...].astype(F32), axis=0, keepdims=True)
 
     ph_c1.wait_recv()
@@ -712,6 +824,18 @@
     sg[2:3, :] = jnp.sum(gab, axis=0, keepdims=True)
     gab = gab.astype(BF)
     gabp[...] = dot_nn(spread, gab).astype(BF)
+    for tile in range(tiles):
+        ga[3, TILE * tile : TILE * (tile + 1), :] = dot_tn(
+            attn[:, TILE * tile : TILE * (tile + 1)], gab
+        ).astype(BF)
+
+    core_copies, x_copies = [], []
+
+    def to_core_sum(source, landing, k):
+        core_copies.append(send(source, landing, sem_as.at[k, 0], sem_ar.at[k, 0], to_core))
+
+    to_core_sum(ga.at[3, :, her_cols], rca.at[3], 2)
+    sum_fc2[1].middle()
 
     dbias[...] = jnp.zeros_like(dbias)
     dh1[...] = jnp.zeros_like(dh1)
@@ -742,33 +866,21 @@
             dh1[...] += dot_nn(grads[tile], wa[s, cols, :])
         sg[6:7, cols] = jnp.sum(dqs[tile].astype(F32), axis=0, keepdims=True)
         sg[7:8, cols] = jnp.sum(dvs[tile].astype(F32), axis=0, keepdims=True)
-        attn_tile = dot_nn(gather, at[tile]).astype(BF)
-        ga[3, cols, :] = dot_tn(attn_tile, gab).astype(BF)
         return carry
 
     half_rows = width // 2
     halves = [pl.ds(0, half_rows), pl.ds(half_rows, half_rows)]
-    core_copies, x_copies = [], []
+
+    def add_core(slot, part):
+        add_to(ga.at[slot, part, my_cols], rca.at[slot, part, :])
 
     def reduce_core(half):
-        core_copies.append(
-            send(
-                ga.at[:, halves[half], her_cols],
-                rca.at[:, halves[half], :],
-                sem_as.at[half, 0],
-                sem_ar.at[half, 0],
-                to_core,
-            )
-        )
-
-    def add_core(slot, part):
-        ga[slot, part, my_cols] = (
-            ga[slot, part, my_cols].astype(F32) + rca[slot, part, :].astype(F32)
-        ).astype(BF)
+        part = halves[half]
+        to_core_sum(ga.at[pl.ds(0, 3), part, her_cols], rca.at[pl.ds(0, 3), part, :], half)
 
     def reduce_x(half):
         part = halves[half]
-        core_copies[half].wait_recv()
+        core_copies[1 + half].wait_recv()
         add_core(far, part)
         x_copies.append(
             send(
@@ -779,38 +891,41 @@
                 to_x,
             )
         )
-        add_core(3, part)
-        scatter_y(2, half)
         add_core(1, part)
-        scatter_y(1, half)
+        sum_key.scatter(half)
         add_core(near, part)
 
     lax.fori_loop(0, tiles_half, attend_back, 0)
     reduce_core(0)
-    lax.fori_loop(0, tiles, fc1_grad, 0)
-    scatter_y(3, 0)
-    scatter_y(3, 1)
+    core_copies[0].wait_recv()
+    add_core(3, slice(None))
+    sum_proj.scatter(0)
+    sum_proj.scatter(1)
     reduce_x(0)
-    scatter_z(4)
+    sum_fc2[0].start_z()
     lax.fori_loop(tiles_half, tiles, attend_back, 0)
     reduce_core(1)
 
     def mlp_out(slot):
         ph[slot] = dot_nn(ac[slot_rows(slot), :], wf[1]).astype(BF)
+
+    def near_y(half):
+        x_copies[half].wait_recv()
+        add_to(ga.at[near, halves[half], my_cols], rxa.at[halves[half]])
+        sum_near.scatter(half)
 
     out_copies = []
     sent(ph_c0)
     sent(ph_c1)
     mlp_out(xc_dl)
     out_copies.append(send(ph.at[xc_dl], rc_o.at[0], sem_hs.at[1, 0], sem_hr.at[1, 0], to_core))
+    reduce_x(1)
     mlp_out(core_dl)
     out_copies.append(send(ph.at[core_dl], rc_o.at[1], sem_hs.at[1, 1], sem_hr.at[1, 1], to_core))
-    reduce_x(1)
     mlp_out(x_dl)
-    out_copies[0].wait_recv()
-    ph2[1] = (ph[x_dl].astype(F32) + rc_o[0].astype(F32)).astype(BF)
-    out_copies.append(send(ph2.at[1], rx_o, sem_hs.at[1, 2], sem_hr.at[1, 2], to_x))
-    mlp_out(mine)
+    near_y(0)
+    sum_fc2[0].middle()
+    sum_fc2[1].start_y()
 
     dh1c = dot_nn(gather, dh1[...].astype(BF))
     n1 = n1s[...]
@@ -839,56 +954,30 @@
             row, spot = 12 + head // heads_here, LANES * (head % heads_here)
             sg[row : row + 1, spot : spot + LANES] = jnp.sum(line, axis=0, keepdims=True)
 
-    def small_start(stage, devices):
-        return stage, [
-            send(sg, sg_in.at[stage + k], sem_ss.at[stage + k], sem_sr.at[stage + k], device)
+    last_small = 1 + z_count + groups
+
+    def small_start(stage, ref, devices):
+        cols = slice(None) if ref is sg else my_cols
+        return ref, [sg_in.at[stage + k, :, cols] for k in range(len(devices))], [
+            send(
+                ref,
+                sg_in.at[stage + k, :, cols],
+                sem_ss.at[stage + k],
+                sem_sr.at[stage + k],
+                device,
+            )
             for k, device in enumerate(devices)
         ]
 
     def small_end(started):
-        stage, copies = started
+        ref, landings, copies = started
         for copy in copies:
             copy.wait_recv()
             sent(copy)
-        total = sg[...]
-        for k in range(len(copies)):
-            total = total + sg_in[stage + k]
-        sg[...] = total
-
-    smalls = small_start(0, [to_core])
-
-    for half in range(2):
-        x_copies[half].wait_recv()
-        part = halves[half]
-        ga[near, part, my_cols] = (
-            ga[near, part, my_cols].astype(F32) + rxa[part, :].astype(F32)
-        ).astype(BF)
-        scatter_y(0, half)
-
-    small_end(smalls)
-    smalls = small_start(1, [to_x])
-
-    out_copies[1].wait_recv()
-    out_copies[2].wait_recv()
-    branch = ph[mine].astype(F32) + rc_o[1].astype(F32) + rx_o[...].astype(F32)
-    out_ref[...] = (x1s[...] + (branch + flat_row(f2b_ref)) * row_live).astype(BF)[0:rows]
-
-    small_end(smalls)
-    smalls = small_start(2, [to_y])
-
-    scatter_z(2)
-    scatter_z(3)
-    small_end(smalls)
-    smalls = small_start(3, [to_z(step) for step in range(1, z_count)])
-    scatter_z(1)
-
-    def total_z(index):
-        landing, far_landing = sums[index][2:]
-        total = landing[z].astype(F32)
-        for step in range(1, z_count):
-            along_z[index, step].wait_recv()
-            total = total + far_landing[step - 1].astype(F32)
-        return total.astype(BF)
+        total = ref[...]
+        for landing in landings:
+            total = total + landing[...]
+        ref[...] = total
 
     def swap(ref, dst, index, device):
         return send(ref, dst, sem_fs.at[index], sem_fr.at[index], device)
@@ -900,42 +989,91 @@
             copy.wait_recv()
             sent(copy)
         if groups > 1:
-            total = ref[...].astype(F32)
-            for step in range(1, groups):
-                total = total + landing[step - 1].astype(F32)
-            ref[...] = total.astype(BF)
+            add_to(ref, *[landing.at[step - 1] for step in range(1, groups)])
 
     final = {}
-    for k, index in enumerate((4, 3)):
-        fin[1 - k, mine] = total_z(index)
-        slot = fin.at[1 - k, mine]
-        over_groups(slot, group_m.at[1 - k], k)
-        final[index, 0] = swap(slot, slot, 3 * k, to_x)
-        final[index, 1] = swap(slot, slot, 3 * k + 1, to_core)
-    for k, (index, slot) in enumerate(((2, 3), (1, 1))):
-        fin_a[slot, :, my_cols] = total_z(index)
-        final[index, 0] = swap(fin_a.at[slot, :, my_cols], fin_x.at[k], 6 + k, to_x)
-    scatter_z(0)
-    for k, index in enumerate((4, 3)):
-        final[index, 0].wait_recv()
-        slot = fin.at[1 - k, x_dl]
-        final[index, 2] = swap(slot, slot, 3 * k + 2, to_core)
-    for index in (4, 3):
-        final[index, 1].wait_recv()
-        final[index, 2].wait_recv()
-    fin_ref[1] = fin[0]
-    fin_ref[2] = fin[1]
-    for k, (index, slot) in enumerate(((2, 3), (1, 1))):
-        final[index, 0].wait_recv()
-        sent(final[index, 0])
-        fin_a[slot, :, my_cols] = (
-            fin_a[slot, :, my_cols].astype(F32) + fin_x[k].astype(F32)
-        ).astype(BF)
-        over_groups(fin_a.at[slot, :, my_cols], group_a.at[k], 2 + k)
-
+
+    def finish(which, parts):
+        for part, cols in zip(parts, (left_cols, right_cols), strict=True):
+            fin[which, mine, :, cols] = part.total()[...]
+        slot = fin.at[which, mine]
+        over_groups(slot, group_m.at[which], which)
+        final[which, 0] = swap(slot, slot, 3 * which, to_x)
+        final[which, 1] = swap(slot, slot, 3 * which + 1, to_core)
+
+    def finish_core(which):
+        final[which, 0].wait_recv()
+        slot = fin.at[which, x_dl]
+        final[which, 2] = swap(slot, slot, 3 * which + 2, to_core)
+
+    def finish_out(which):
+        final[which, 1].wait_recv()
+        final[which, 2].wait_recv()
+        fin_ref[1 + which] = fin[which]
+
+    def share_x(k, slot, part):
+        fin_a[slot, :, my_cols] = part.total()[...]
+        final[2, k] = swap(fin_a.at[slot, :, my_cols], fin_x.at[k], 6 + k, to_x)
+
+    def shared_x(k, slot):
+        final[2, k].wait_recv()
+        sent(final[2, k])
+        ref = fin_a.at[slot, :, my_cols]
+        add_to(ref, fin_x.at[k])
+        over_groups(ref, group_a.at[k], 2 + k)
+
+    smalls = small_start(0, sg, [to_core])
+    for part in sum_fc1:
+        part.start_z()
+    near_y(1)
+    small_end(smalls)
+    smalls = small_start(1, sg, [to_x])
+    out_copies[0].wait_recv()
+    ph2[1] = (ph[x_dl].astype(F32) + rc_o[0].astype(F32)).astype(BF)
+    out_copies.append(send(ph2.at[1], rx_o, sem_hs.at[1, 2], sem_hr.at[1, 2], to_x))
+    mlp_out(mine)
+    small_end(smalls)
+    sg_half = sg.at[:, my_cols]
+    smalls = small_start(2, sg_half, [to_y])
+    sum_proj.start_z()
+    for part in sum_fc1:
+        part.middle()
+    finish(1, sum_fc2)
+    small_end(smalls)
+    smalls = small_start(3, sg_half, [to_z(step) for step in range(1, z_count)])
+    sum_key.start_z()
+    sum_proj.middle()
+    finish(0, sum_fc1)
+    finish_core(1)
+
+    out_copies[1].wait_recv()
+    out_copies[2].wait_recv()
+    branch = ph[mine].astype(F32) + rc_o[1].astype(F32) + rx_o[...].astype(F32)
+    out_ref[...] = (x1s[...] + (branch + flat_row(f2b_ref)) * row_live).astype(BF)[0:rows]
+
+    sum_key.middle()
     small_end(smalls)
     if groups > 1:
-        small_end(small_start(2 + z_count, [to_group(step) for step in range(1, groups)]))
+        small_end(
+            small_start(
+                2 + z_count, sg_half, [to_group(step) for step in range(1, groups)]
+            )
+        )
+    small_last = send(
+        sg_half,
+        sg_in.at[last_small, :, my_cols],
+        sem_ss.at[last_small],
+        sem_sr.at[last_small],
+        to_core,
+    )
+    sum_near.start_z()
+    share_x(0, 3, sum_proj)
+    finish_core(0)
+    share_x(1, 1, sum_key)
+    small_last.wait_recv()
+    sg[:, her_cols] = sg_in[last_small, :, her_cols]
+    finish_out(1)
+    shared_x(0, 3)
 
     vec_ref[...] = sg[0:8, :]
     pick = one_hot(iota((width, block), 0) == block * mp + iota((width, block), 1), F32)
@@ -958,7 +1096,9 @@
     turn = one_hot(iota((LANES, LANES), 0) + iota((LANES, LANES), 1) == LANES - 1, F32)
     small_ref[16:24, 0:LANES] = dot_nn(table, turn, HIGHEST)
 
-    fin_a[near, :, my_cols] = total_z(0)
+    finish_out(0)
+    shared_x(1, 1)
+    fin_a[near, :, my_cols] = sum_near.total()[...]
     slot = fin_a.at[near, :, my_cols]
     over_groups(slot, group_a.at[2], 4)
     near_x = swap(slot, slot, 8, to_x)
@@ -1101,10 +1241,9 @@
                 pltpu.VMEM((2, width, width), BF),
                 pltpu.VMEM((GROUP, width, width // 2), BF),
                 pltpu.VMEM((width, width // 2), BF),
-                pltpu.VMEM((3, z_count, block, width // 2), BF),
-                pltpu.VMEM((3, z_count - 1, block, width // 2), BF),
-                pltpu.VMEM((2, z_count, block, width), BF),
-                pltpu.VMEM((2, z_count - 1, block, width), BF),
+                pltpu.VMEM((7, z_count, block, width // 2), BF),
+                pltpu.VMEM((8, z_count - 1, block, width // 2), BF),
+                pltpu.VMEM((8, block, width // 2), BF),
                 pltpu.VMEM((2, GROUP, block, width), BF),
                 pltpu.VMEM((GROUP, block, width), BF),
                 pltpu.VMEM((2, block, width // 2), BF),
@@ -1120,12 +1259,12 @@
                 dma((2, 3)),
                 dma((2, 3)),
                 dma((2, 3)),
-                dma((2, 2)),
-                dma((2, 2)),
-                dma((5, z_count)),
-                dma((5, z_count)),
-                dma((5, z_count)),
-                dma((5, z_count)),
+                dma((3, 2)),
+                dma((3, 2)),
+                dma((7, z_count)),
+                dma((7, z_count)),
+                dma((8, 4)),
+                dma((8, 4)),
                 dma((10,)),
                 dma((10,)),
                 dma((2 + z_count + groups,)),

time: 155 us -> 138 us (0.89)
  Pallas kernels: 154 us -> 137 us
    pallas_call x1, Pallas kernels: 150 us -> 133 us  [shards(): pl.pallas_call(functools.partial(body, dims), out_shape=[jax.ShapeDtypeSt...]
where the time goes in v3:
time: 138 us
  Pallas kernels  137 us (99%)
    pallas_call x1, Pallas kernels, shards(): pl.pallas_call(functools.partial(body, dims), out_shape=[jax.ShapeDtypeSt...  133 us
    pallas_call x1, Pallas kernels, shards(): pl.pallas_call(unpack, out_shape=[jax.ShapeDtypeStruct((rows, width), BF)...  3.9 us

profile of v3, /device:TPU:1, one launch (start us, length us, event | category | flops | bytes accessed | tf_op | source)
XLA Modules:
  0.0 137.7 jit_solution(10968775004914303864)
XLA Ops:
  0.7 133.0 %shard_map.271 = (bf16[147,768]{1,0:T(8,128)(2,1)}, bf16[147,768]{1,0:T(8,128)(2,1)}, f32[8,768]{1,0:T(8,128)}, f32[24,384]{1,0:T(8,128)}, bf16[3,4,96,768]{3,2,1,0:T(8,128)(2,1)}) custom-call(s32[24]{0:T(128)} %kind_ref.1, bf16[147,768]{1,0:T(8,128)(2,1)} %tok_ref.1, bf16[147,768]{1,0:T(8,128)(2,1)} %og_ref.1, f32[768]{0:T(1024)} %n1g_ref.1, f32[768]{0:T(1024)} %n1b_ref.1, ...), custom_call_target="tpu_custom_call" | custom-call | tf_op jit(solution)/shard_map/pallas_call | solution.py:1192
  133.6 3.9 %shard_map.272 = (bf16[147,768]{1,0:T(8,128)(2,1)}, bf16[147,768]{1,0:T(8,128)(2,1)}, f32[768]{0:T(1024)}, f32[768]{0:T(1024)}, f32[3,96,768]{2,1,0:T(8,128)}, /...) custom-call(bf16[147,768]{1,0:T(8,128)(2,1)} %get-tuple-element.35.o, ...), custom_call_target="tpu_custom_call" | custom-call | tf_op jit(solution)/shard_map/pallas_call | solution.py:1296

commit v4 on v3

--- a/solution.py
+++ b/solution.py
@@ -781,7 +781,7 @@
             return ref
 
     left_cols, right_cols = pl.ds(0, half_width), pl.ds(half_width, half_width)
-    sum_near = YFirst(0, ga.at[near], my_cols, False)
+    sum_near = YFirst(0, ga.at[near], my_cols, True)
     sum_key = YFirst(1, ga.at[1], my_cols, True)
     sum_proj = YFirst(2, ga.at[3], my_cols, True)
     sum_fc1 = [YFirst(3, gf.at[0], left_cols, True), YFirst(4, gf.at[0], right_cols, True)]
@@ -1069,6 +1069,7 @@
     sum_near.start_z()
     share_x(0, 3, sum_proj)
     finish_core(0)
+    sum_near.middle()
     share_x(1, 1, sum_key)
     small_last.wait_recv()
     sg[:, her_cols] = sg_in[last_small, :, her_cols]

time: 138 us -> 135 us (0.978)
  Pallas kernels: 137 us -> 134 us
    pallas_call x1, Pallas kernels: 133 us -> 130 us  [shards(): pl.pallas_call(functools.partial(body, dims), out_shape=[jax.ShapeDtypeSt...]
where the time goes in v4:
time: 135 us; the launch traced here: 134 us
  Pallas kernels  134 us (99%)
    pallas_call x1, Pallas kernels, shards(): pl.pallas_call(functools.partial(body, dims), out_shape=[jax.ShapeDtypeSt...  130 us
    pallas_call x1, Pallas kernels, shards(): pl.pallas_call(unpack, out_shape=[jax.ShapeDtypeStruct((rows, width), BF)...  3.9 us

profile of v4, /device:TPU:1, one launch (start us, length us, event | category | flops | bytes accessed | tf_op | source)
XLA Modules:
  0.0 134.4 jit_solution(17819382119401974999)
XLA Ops:
  0.7 129.7 %shard_map.271 = (bf16[147,768]{1,0:T(8,128)(2,1)}, bf16[147,768]{1,0:T(8,128)(2,1)}, f32[8,768]{1,0:T(8,128)}, f32[24,384]{1,0:T(8,128)}, bf16[3,4,96,768]{3,2,1,0:T(8,128)(2,1)}) custom-call(s32[24]{0:T(128)} %kind_ref.1, bf16[147,768]{1,0:T(8,128)(2,1)} %tok_ref.1, bf16[147,768]{1,0:T(8,128)(2,1)} %og_ref.1, f32[768]{0:T(1024)} %n1g_ref.1, f32[768]{0:T(1024)} %n1b_ref.1, ...), custom_call_target="tpu_custom_call" | custom-call | tf_op jit(solution)/shard_map/pallas_call | solution.py:1193
  130.3 3.9 %shard_map.272 = (bf16[147,768]{1,0:T(8,128)(2,1)}, bf16[147,768]{1,0:T(8,128)(2,1)}, f32[768]{0:T(1024)}, f32[768]{0:T(1024)}, f32[3,96,768]{2,1,0:T(8,128)}, /...) custom-call(bf16[147,768]{1,0:T(8,128)(2,1)} %get-tuple-element.35.o, ...), custom_call_target="tpu_custom_call" | custom-call | tf_op jit(solution)/shard_map/pallas_call | solution.py:1297

commit v5 on v4

--- a/solution.py
+++ b/solution.py
@@ -473,10 +473,10 @@
     for place in range(z_count):
         forward_proj(proj_w.arrive_y(place))
     gg_x = send_rows(gg, 0, mine, to_x, 0)
+    fc2_long.arrive_y()
+    fc2_long.start_z()
     for place in later_z[1:]:
         fc1_w.arrive_z(place)
-    fc2_long.arrive_y()
-    fc2_long.start_z()
     for place in range(z_count):
         key_w.arrive_y(place)
     core_near = core_half(0, near)

time: 135 us -> 135 us (level)
  no operation moved by 1% of the time
where the time goes in v5:
time: 135 us; the launch traced here: 134 us
  Pallas kernels  134 us (99%)
    pallas_call x1, Pallas kernels, shards(): pl.pallas_call(functools.partial(body, dims), out_shape=[jax.ShapeDtypeSt...  130 us
    pallas_call x1, Pallas kernels, shards(): pl.pallas_call(unpack, out_shape=[jax.ShapeDtypeStruct((rows, width), BF)...  3.9 us

profile of v5, /device:TPU:1, one launch (start us, length us, event | category | flops | bytes accessed | tf_op | source)
XLA Modules:
  0.0 134.4 jit_solution(4817927245369592814)
XLA Ops:
  0.7 129.7 %shard_map.271 = (bf16[147,768]{1,0:T(8,128)(2,1)}, bf16[147,768]{1,0:T(8,128)(2,1)}, f32[8,768]{1,0:T(8,128)}, f32[24,384]{1,0:T(8,128)}, bf16[3,4,96,768]{3,2,1,0:T(8,128)(2,1)}) custom-call(s32[24]{0:T(128)} %kind_ref.1, bf16[147,768]{1,0:T(8,128)(2,1)} %tok_ref.1, bf16[147,768]{1,0:T(8,128)(2,1)} %og_ref.1, f32[768]{0:T(1024)} %n1g_ref.1, f32[768]{0:T(1024)} %n1b_ref.1, ...), custom_call_target="tpu_custom_call" | custom-call | tf_op jit(solution)/shard_map/pallas_call | solution.py:1193
  130.3 3.9 %shard_map.272 = (bf16[147,768]{1,0:T(8,128)(2,1)}, bf16[147,768]{1,0:T(8,128)(2,1)}, f32[768]{0:T(1024)}, f32[768]{0:T(1024)}, f32[3,96,768]{2,1,0:T(8,128)}, /...) custom-call(bf16[147,768]{1,0:T(8,128)(2,1)} %get-tuple-element.35.o, ...), custom_call_target="tpu_custom_call" | custom-call | tf_op jit(solution)/shard_map/pallas_call | solution.py:1297
